TPU v7x, 256 devices: a whole 4x4x8 slice. The times are simulated.
256 devices in a mesh: dp: 16 (over z_lo, y, core), space: 16 (over x, z_hi).
Axes of the slice: x: 4, y: 4, z: 8 (z_hi: 4, z_lo: 2; z = z_hi * 2 + z_lo), core: 2. Of those that a mesh axis runs over, the one named last changes fastest.
Arguments:
- cotangent: bfloat16 [16, 96, 368, 768], P('dp', None, 'space'), may hold values from -6 to 6
- spectrum: bfloat16 [16, 2, 96, 368, 368], P('dp', None, None, 'space'), may hold values from -6 to 6
- first_weight: bfloat16 [2, 1, 96, 96], replicated, may hold values from -0.4375 to 0.4375
- first_bias: bfloat16 [2, 1, 96], replicated, may hold values from -3 to 3
- second_weight: bfloat16 [2, 1, 96, 96], replicated, may hold values from -0.4375 to 0.4375
- second_bias: bfloat16 [2, 1, 96], replicated, may hold values from -3 to 3
Outputs:
- grad_input: bfloat16 [16, 96, 368, 768], P('dp', None, 'space')
- grad_first_weight: float32 [2, 1, 96, 96], P(None, None, 'dp')
- grad_first_bias: float32 [2, 1, 96], P(None, None, 'dp')
- grad_second_weight: float32 [2, 1, 96, 96], P(None, None, 'dp')
- grad_second_bias: float32 [2, 1, 96], P(None, None, 'dp')
All inputs are finite; a program needn't handle non-finite values.
Results may differ from a plain program's by a relative error of at most 0.011.
The roundings to bfloat16 on the way count: a program that leaves them out, or rounds other values in their place, can miss the bound.
Values may be sent and summed in bfloat16 or wider, within the bound.
A program may use at most 128 MiB of HBM per device.

v0:
```python
import math

import jax
import jax.numpy as jnp
from jax import lax
from jax.sharding import PartitionSpec as P

H = 368
W = 768
KW = 368
BS = 96
BLOCKS = 1
C = 96


def angle_tables(n, rows, cols):
    index = (
        jnp.arange(rows, dtype=jnp.int32)[:, None] * jnp.arange(cols, dtype=jnp.int32)[None, :] % n
    )
    theta = index.astype(jnp.float32) * (2.0 * math.pi / n)
    return (jnp.cos(theta).astype(jnp.bfloat16), jnp.sin(theta).astype(jnp.bfloat16))


def mix_fwd(inputs, weight):
    return jnp.einsum("bckp,bcd->bdkp", inputs, weight, preferred_element_type=jnp.float32)


def mix_back(inputs, weight):
    return jnp.einsum("bdkp,bcd->bckp", inputs, weight, preferred_element_type=jnp.float32)


def outer_sum(left, right):
    return jnp.einsum("bckp,bdkp->bcd", left, right, preferred_element_type=jnp.float32)


def contract(left, table, form):
    return jnp.einsum(form, left, table, preferred_element_type=jnp.float32)


def on_device(cotangent, spectrum, first_weight, first_bias, second_weight, second_bias):
    grad_out = cotangent[0]
    saved = spectrum[0]
    local_modes = saved.shape[2]
    local_lats = grad_out.shape[1]
    groups = lax.axis_size("space")
    lon_cos, lon_sin = angle_tables(W, W, KW)
    lat_cos, lat_sin = angle_tables(H, H, H)
    scale = 1.0 / math.sqrt(H * W)
    wave_index = lax.axis_index("space") * local_modes + jnp.arange(local_modes, dtype=jnp.int32)
    mult = jnp.where(wave_index == 0, 1.0, 2.0).astype(jnp.float32) * scale
    lon_table = jnp.stack([lon_cos, -lon_sin]).reshape(2, W, groups, local_modes)
    longitude = contract(grad_out, lon_table, "chw,swnk->scnhk").astype(jnp.bfloat16)
    longitude = longitude.reshape(2, C, groups, local_lats * local_modes)
    pieces = lax.all_to_all(longitude, "space", split_axis=2, concat_axis=2, tiled=True)
    items = pieces.shape[1]
    grid = pieces.reshape(2, items, H, local_modes)
    part_re = grid[0]
    part_im = grid[1]
    out_re = contract(part_re, lat_cos, "chk,hp->ckp") + contract(part_im, lat_sin, "chk,hp->ckp")
    out_im = contract(part_im, lat_cos, "chk,hp->ckp") - contract(part_re, lat_sin, "chk,hp->ckp")
    dz_all = jnp.stack([out_re, out_im]) * mult[None, None, :, None]
    dz_all = dz_all.reshape(2, BLOCKS, BS, local_modes, H)
    y_all = saved.reshape(2, BLOCKS, BS, local_modes, H)
    y_re, y_im = (y_all[0], y_all[1])
    w1r, w1i = (first_weight[0], first_weight[1])
    w2r, w2i = (second_weight[0], second_weight[1])
    b1 = first_bias.astype(jnp.float32)[:, :, :, None, None]
    b2 = second_bias.astype(jnp.float32)[:, :, :, None, None]
    u_re = mix_fwd(y_re, w1r) - mix_fwd(y_im, w1i) + b1[0]
    u_im = mix_fwd(y_re, w1i) + mix_fwd(y_im, w1r) + b1[1]
    a_re = jnp.maximum(u_re, 0.0).astype(jnp.bfloat16)
    a_im = jnp.maximum(u_im, 0.0).astype(jnp.bfloat16)
    v_re = mix_fwd(a_re, w2r) - mix_fwd(a_im, w2i) + b2[0]
    v_im = mix_fwd(a_re, w2i) + mix_fwd(a_im, w2r) + b2[1]
    dv_re = jnp.where(jnp.abs(v_re) > 0.01, dz_all[0], 0.0).astype(jnp.bfloat16)
    dv_im = jnp.where(jnp.abs(v_im) > 0.01, dz_all[1], 0.0).astype(jnp.bfloat16)
    gw2 = jnp.stack(
        [
            outer_sum(a_re, dv_re) + outer_sum(a_im, dv_im),
            outer_sum(a_re, dv_im) - outer_sum(a_im, dv_re),
        ]
    )
    gb2 = jnp.stack(
        [
            jnp.sum(dv_re, axis=(2, 3), dtype=jnp.float32),
            jnp.sum(dv_im, axis=(2, 3), dtype=jnp.float32),
        ]
    )
    da_re = mix_back(dv_re, w2r) + mix_back(dv_im, w2i)
    da_im = mix_back(dv_im, w2r) - mix_back(dv_re, w2i)
    du_re = jnp.where(u_re > 0.0, da_re, 0.0).astype(jnp.bfloat16)
    du_im = jnp.where(u_im > 0.0, da_im, 0.0).astype(jnp.bfloat16)
    gw1 = jnp.stack(
        [
            outer_sum(y_re, du_re) + outer_sum(y_im, du_im),
            outer_sum(y_re, du_im) - outer_sum(y_im, du_re),
        ]
    )
    gb1 = jnp.stack(
        [
            jnp.sum(du_re, axis=(2, 3), dtype=jnp.float32),
            jnp.sum(du_im, axis=(2, 3), dtype=jnp.float32),
        ]
    )
    dy_re = (
        (mix_back(du_re, w1r) + mix_back(du_im, w1i))
        .astype(jnp.bfloat16)
        .reshape(C, local_modes, H)
    )
    dy_im = (
        (mix_back(du_im, w1r) - mix_back(du_re, w1i))
        .astype(jnp.bfloat16)
        .reshape(C, local_modes, H)
    )
    q_re = contract(dy_re, lat_cos, "ckp,ph->chk") - contract(dy_im, lat_sin, "ckp,ph->chk")
    q_im = contract(dy_re, lat_sin, "ckp,ph->chk") + contract(dy_im, lat_cos, "ckp,ph->chk")
    latitude = (
        jnp.stack([q_re, q_im]).astype(jnp.bfloat16).reshape(2, C, groups, local_lats * local_modes)
    )
    returned = lax.all_to_all(latitude, "space", split_axis=2, concat_axis=2, tiled=True)
    returned = returned.reshape(2, C, groups, local_lats, local_modes)
    back_table = jnp.stack([lon_cos, -lon_sin]).reshape(2, W, groups, local_modes)
    back = contract(returned, back_table, "scnhk,swnk->chw")
    grad_in = (grad_out.astype(jnp.float32) + scale * back).astype(jnp.bfloat16)[None]
    totals = lax.psum((gw1, gb1, gw2, gb2), "space")
    gw1, gb1, gw2, gb2 = (
        lax.psum_scatter(totals[0], "dp", scatter_dimension=2, tiled=True),
        lax.psum_scatter(totals[1], "dp", scatter_dimension=2, tiled=True),
        lax.psum_scatter(totals[2], "dp", scatter_dimension=2, tiled=True),
        lax.psum_scatter(totals[3], "dp", scatter_dimension=2, tiled=True),
    )
    return (grad_in, gw1, gb1, gw2, gb2)


def solution(mesh):
    in_specs = (
        P("dp", None, "space", None),
        P("dp", None, None, "space", None),
        P(),
        P(),
        P(),
        P(),
    )
    out_specs = (
        P("dp", None, "space", None),
        P(None, None, "dp", None),
        P(None, None, "dp"),
        P(None, None, "dp", None),
        P(None, None, "dp"),
    )
    return jax.shard_map(
        on_device, mesh=mesh, in_specs=in_specs, out_specs=out_specs, check_vma=False
    )
```

profile of v0, /device:TPU:32, one launch (start us, length us, event | category | flops | bytes accessed | tf_op | source)
XLA Modules:
  0.0 504.3 jit_solution(7841108493731889977)
XLA Ops:
  7.2 4.9 fusion.85
  12.1 4.8 cosine_convert_fusion
  16.9 5.8 %convert_bitcast_fusion = bf16[2,96,16,23,23]{1,4,3,2,0:T(8,128)(2,1)S(1)} fusion(bf16[1,96,23,768]{3,1,2,0:T(8,128)(2,1)} %param.6, bf16[1,768,16,23]{1,3,2,0:T(8,128)(2,1)S(1)} %fusion.85, bf16[1,768,16,23]{1,3,2,0:T(8,128)(2,1)S(1)} %cosine_convert_fusion), kind=kOutput, calls=%fused_computation.4 | convolution fusion | flops 2500021248 | bytes 7772160 | tf_op jit(solution)/shard_map/chw,swnk->scnhk/dot_general | solution.py:37
  25.4 8.2 %copy.57 = bf16[2,96,16,529]{3,1,0,2:T(8,128)(2,1)} copy(bf16[2,96,16,529]{1,2,3,0:T(8,128)(2,1)} %bitcast.316) | data formatting | bytes 6500352 | tf_op jit(solution)/shard_map/reshape | solution.py:53
  33.6 10.6 %all-to-all-start = ((bf16[2,96,16,529]{3,1,0,2:T(8,128)(2,1)}), bf16[2,96,16,529]{3,1,0,2:T(8,128)(2,1)}, u32[]{:S(2)}, u32[]{:S(2)}) async-start(bf16[2,96,16,529]{3,1,0,2:T(8,128)(2,1)} %copy.57), calls=%async_computation | async-start | bytes 7864320 | tf_op jit(solution)/shard_map/all_to_all | solution.py:54
  55.5 77.5 %all-to-all-done = bf16[2,96,16,529]{3,1,0,2:T(8,128)(2,1)} async-done(((bf16[2,96,16,529]{3,1,0,2:T(8,128)(2,1)}), bf16[2,96,16,529]{3,1,0,2:T(8,128)(2,1)}, u32[]{:S(2)}, u32[]{:S(2)}) %all-to-all-start) | async-done | bytes 3250208 | tf_op jit(solution)/shard_map/all_to_all | solution.py:54
  133.0 4.5 fusion.167
  137.4 4.0 copy.58
  141.4 4.2 squeeze.11
  145.6 4.1 copy.59
  149.7 4.0 copy.60
  153.7 4.2 squeeze.12
  157.9 4.3 copy.61
  162.2 4.6 fusion.99
  166.8 3.0 fusion.101
  169.8 3.0 subtract_bitcast_fusion
  172.9 3.5 add_bitcast_fusion
  193.0 4.8 fusion.19
  199.6 4.6 fusion.38
  204.2 4.2 copy.73
  208.4 4.2 stack.67
  212.6 6.6 %fusion.35 = bf16[96,368,23]{1,0,2:T(8,128)(2,1)} fusion(f32[368,96,23]{0,1,2:T(8,128)} %fusion.19, bf16[23,368,96]{1,2,0:T(8,128)(2,1)} %copy-done.5), kind=kOutput, calls=%fused_computation.63 | convolution fusion | flops 601011712 | bytes 6500352 | tf_op jit(solution)/shard_map/ckp,ph->chk/dot_general | solution.py:37
  219.2 4.1 copy.72
  223.3 4.2 stack.66
  227.5 5.4 %pad_maximum_fusion = bf16[2,96,16,529]{1,3,2,0:T(8,128)(2,1)} fusion(bf16[1,96,16,529]{1,3,2,0:T(8,128)(2,1)} %stack.67, bf16[1,96,16,529]{1,3,2,0:T(8,128)(2,1)} %stack.66), kind=kLoop, calls=%fused_computation.5 | loop fusion | flops 1625088 | bytes 6500352 | tf_op jit(solution)/shard_map/stack | solution.py:118
  232.9 6.6 %copy.74 = bf16[2,96,16,529]{3,1,0,2:T(8,128)(2,1)} copy(bf16[2,96,16,529]{1,3,2,0:T(8,128)(2,1)} %pad_maximum_fusion) | data formatting | bytes 6500352 | tf_op jit(solution)/shard_map/stack | solution.py:118
  239.4 7.0 %all-to-all-start.1 = ((bf16[2,96,16,529]{3,1,0,2:T(8,128)(2,1)}), bf16[2,96,16,529]{3,1,0,2:T(8,128)(2,1)}, u32[]{:S(2)}, u32[]{:S(2)}) async-start(bf16[2,96,16,529]{3,1,0,2:T(8,128)(2,1)} %copy.74), calls=%async_computation.1 | async-start | bytes 7864320 | tf_op jit(solution)/shard_map/all_to_all | solution.py:120
  259.9 94.9 %all-reduce.5 = (f32[2,1,96]{2,1,0:T(1,128)S(1)}, f32[2,1,96]{2,1,0:T(1,128)S(1)}) all-reduce(f32[2,1,96]{2,1,0:T(1,128)S(1)} %pad_maximum_fusion.5, f32[2,1,96]{2,1,0:T(1,128)S(1)} %pad_maximum_fusion.6), channel_id=3, replica_groups=mesh['dp'=16,'space'=16] {'dp'}, use_global_device_ids=true, to_apply=%region_5.6.clone | all-reduce | flops 384 | bytes 3072
  354.9 41.7 %all-reduce.9.cloned.1.call-done = (f32[2,1,96,96]{3,0,1,2:T(2,128)}, f32[2,1,96,96]{3,0,1,2:T(2,128)}) async-done(((f32[2,1,96,96]{3,0,1,2:T(2,128)}, f32[2,1,96,96]{3,0,1,2:T(2,128)}), (f32[2,1,96,96]{3,0,1,2:T(2,128)}, f32[2,1,96,96]{3,0,1,2:T(2,128)})) %all-reduce.9.cloned.1.call-update) | async-done | bytes 147472
  397.3 83.2 %all-reduce.4 = (f32[2,1,6,96]{3,0,1,2:T(2,128)S(1)}, f32[2,1,6]{2,1,0:T(1,128)}, f32[2,1,6,96]{3,0,1,2:T(2,128)S(1)}, f32[2,1,6]{2,1,0:T(1,128)}) all-reduce(f32[2,1,6,96]{3,0,1,2:T(2,128)S(1)} %get-tuple-element.47, f32[2,1,6]{2,1,0:T(1,128)S(1)} %get-tuple-element.49, ...), channel_id=1, replica_groups=mesh['dp'=16,'space'=16] {'space'}, use_global_device_ids=true, to_apply=%region_0.1 | all-reduce | flops 2328 | bytes 18624 | tf_op jit(solution)/shard_map/psum | solution.py:125
  481.7 8.3 %copy.75 = bf16[2,96,16,529]{1,2,3,0:T(8,128)(2,1)} copy(bf16[2,96,16,529]{3,1,0,2:T(8,128)(2,1)} %all-to-all-done.1) | data formatting | bytes 6500352 | tf_op jit(solution)/shard_map/all_to_all | solution.py:120
  490.0 7.2 %fusion.2 = bf16[1,96,23,768]{3,1,2,0:T(8,128)(2,1)} fusion(bf16[1,96,23,768]{3,1,2,0:T(8,128)(2,1)S(1)} %copy-done.18, bf16[2,96,16,23,23]{1,2,4,3,0:T(8,128)(2,1)} %bitcast.315, bf16[2,768,16,23,1]{1,3,2,0,4:T(8,128)(2,1)} %fusion.84), kind=kOutput, calls=%fused_computation.6 | convolution fusion | flops 2502918144 | bytes 11163648 | tf_op jit(solution)/shard_map/scnhk,swnk->chw/dot_general | solution.py:37
  (106 shorter events, 46.6 us)
Async XLA Ops:
  12.1 10.6 %copy-start.19 = (bf16[1,768,16,23]{1,3,2,0:T(8,128)(2,1)}, bf16[1,768,16,23]{1,3,2,0:T(8,128)(2,1)S(1)}, u32[]{:S(2)}) copy-start(bf16[1,768,16,23]{1,3,2,0:T(8,128)(2,1)S(1)} %fusion.85) | copy-start | bytes 1695748
  16.9 5.8 %copy-start.20 = (bf16[1,768,16,23]{1,3,2,0:T(8,128)(2,1)}, bf16[1,768,16,23]{1,3,2,0:T(8,128)(2,1)S(1)}, u32[]{:S(2)}) copy-start(bf16[1,768,16,23]{1,3,2,0:T(8,128)(2,1)S(1)} %cosine_convert_fusion) | copy-start | bytes 1695748
  33.6 10.7 %copy-start.25 = (bf16[2,1,96]{2,0,1:T(2,128)(2,1)S(1)}, bf16[2,1,96]{2,0,1:T(2,128)(2,1)}, u32[]{:S(2)}) copy-start(bf16[2,1,96]{2,0,1:T(2,128)(2,1)} %param.9) | copy-start | bytes 1156
  33.6 10.7 %copy-start.26 = (bf16[2,1,96]{2,0,1:T(2,128)(2,1)S(1)}, bf16[2,1,96]{2,0,1:T(2,128)(2,1)}, u32[]{:S(2)}) copy-start(bf16[2,1,96]{2,0,1:T(2,128)(2,1)} %param.11) | copy-start | bytes 1156
  33.6 10.7 %copy-start = (bf16[1,2,96,23,368]{4,2,3,1,0:T(8,128)(2,1)S(1)}, bf16[1,2,96,23,368]{4,2,3,1,0:T(8,128)(2,1)}, u32[]{:S(2)}) copy-start(bf16[1,2,96,23,368]{4,2,3,1,0:T(8,128)(2,1)} %param.7) | copy-start | bytes 9750532
  33.6 10.7 %copy-start.21 = (bf16[2,1,96,96]{3,2,1,0:T(8,128)(2,1)S(1)}, bf16[2,1,96,96]{3,2,1,0:T(8,128)(2,1)}, u32[]{:S(2)}) copy-start(bf16[2,1,96,96]{3,2,1,0:T(8,128)(2,1)} %param.8) | copy-start | bytes 110596
  33.6 99.3 %all-to-all-start = ((bf16[2,96,16,529]{3,1,0,2:T(8,128)(2,1)}), bf16[2,96,16,529]{3,1,0,2:T(8,128)(2,1)}, u32[]{:S(2)}, u32[]{:S(2)}) async-start(bf16[2,96,16,529]{3,1,0,2:T(8,128)(2,1)} %copy.57), calls=%async_computation | async-start | bytes 7864320 | tf_op jit(solution)/shard_map/all_to_all | solution.py:54
  49.4 3.7 copy-start.1
  49.4 1.3 copy-start.22
  162.2 4.6 copy-start.14
  169.8 3.1 copy-start.15
  176.4 1.5 copy-start.3
  176.4 2.5 copy-start.17
  180.3 4.7 copy-start.6
  180.3 2.6 copy-start.16
  184.4 2.8 copy-start.8
  184.4 1.1 copy-start.23
  186.6 2.8 copy-start.10
  186.6 1.1 copy-start.24
  188.8 9.0 %copy-start.12 = (bf16[96,23,368]{2,0,1:T(8,128)(2,1)}, bf16[96,23,368]{2,0,1:T(8,128)(2,1)S(1)}, u32[]{:S(2)}) copy-start(bf16[96,23,368]{2,0,1:T(8,128)(2,1)S(1)} %get-tuple-element.41) | copy-start | bytes 4875268
  198.5 1.2 copy-start.5
  239.4 7.0 %copy-start.27 = (u32[256]{0:T(256)S(1)}, u32[256]{0:T(256)}, u32[]{:S(2)}) copy-start(u32[256]{0:T(256)} %constant.52) | copy-start | bytes 3076
  239.4 242.2 %all-to-all-start.1 = ((bf16[2,96,16,529]{3,1,0,2:T(8,128)(2,1)}), bf16[2,96,16,529]{3,1,0,2:T(8,128)(2,1)}, u32[]{:S(2)}, u32[]{:S(2)}) async-start(bf16[2,96,16,529]{3,1,0,2:T(8,128)(2,1)} %copy.74), calls=%async_computation.1 | async-start | bytes 7864320 | tf_op jit(solution)/shard_map/all_to_all | solution.py:120
  246.4 150.2 %all-reduce.9.cloned.1.call-start = ((), (), s32[]{:S(2)}) async-start(), calls=%async_computation.2 | async-start | bytes 393216
  247.7 2.5 copy-start.4
  250.2 2.2 copy-start.9
  252.4 1.5 copy-start.2
  252.5 2.0 copy-start.7
  255.0 1.5 copy-start.13
  255.7 1.6 copy-start.11
  481.6 8.3 %copy-start.18 = (bf16[1,96,23,768]{3,1,2,0:T(8,128)(2,1)S(1)}, bf16[1,96,23,768]{3,1,2,0:T(8,128)(2,1)}, u32[]{:S(2)}) copy-start(bf16[1,96,23,768]{3,1,2,0:T(8,128)(2,1)} %param.6) | copy-start | bytes 10174468
Sparse Core Ops, SparseCore 0:
  260.0 136.5 all-reduce.8
where the time goes:
time: 510 us; the launch traced here: 504 us
  blocking collectives  178 us (35%)
  waiting for transfers between devices  119 us (23%)
  local copies, waits for them, and re-layouts  82.9 us (16%)
  matrix products  70 us (14%)
  other arithmetic  20.9 us (4%)
  starting transfers between devices  17.7 us (3%)
  between operations  15.5 us (3%)
    unnamed x1, blocking collectives  94.9 us
    psum x1, blocking collectives, on_device(): totals = lax.psum((gw1, gb1, gw2, gb2), 'space')  83.2 us
    all_to_all x1, waiting for transfers between devices, on_device(): lax.all_to_all(longitude, 'space', split_axis=2, concat_axis=2, tiled=True)  77.5 us
    dot_general x10, matrix products, contract(): return jnp.einsum(form, left, table, preferred_element_type=jnp.float32)  46.1 us
    unnamed x2, waiting for transfers between devices  41.7 us
    another operation x3, local copies, waits for them, and re-layouts, on_device(): jnp.stack([q_re, q_im]).astype(jnp.bfloat16)  14.9 us
    dot_general x8, matrix products, mix_fwd(): jnp.einsum('bckp,bcd->bdkp', inputs, weight, preferred_element_type=jnp.f...  11.6 us
    all_to_all x1, starting transfers between devices, on_device(): lax.all_to_all(longitude, 'space', split_axis=2, concat_axis=2, tiled=True)  10.6 us
  transfers between devices with their start and end apart: 3, of which 2 were waited for; matrix products, arithmetic and copies ran while one was open for 5% of the time, Pallas kernels for 0%

commit v1 on v0

v1 whole, which is shorter than its diff:
```python
import math

import jax
import jax.numpy as jnp
import ml_dtypes
import numpy as np
from jax import lax
from jax.experimental import pallas as pl
from jax.experimental.pallas import tpu as pltpu
from jax.sharding import PartitionSpec as P

H = 368
W = 768
KW = 368
C = 96
G = 16
HL = 23
HP = 24
CP = 128
CH = 3
KC = 8
ROWS = G * 2 * KC
MSG = 2 * HP
PP = 384
SCALE = 1.0 / math.sqrt(H * W)
LAM = 0.01
F32 = jnp.float32
BF16 = jnp.bfloat16
MESH = pl.DeviceIdType.MESH


def angles(n, rows, cols):
    index = (rows[:, None].astype(np.int64) * cols[None, :].astype(np.int64)) % n
    theta = index.astype(np.float32) * np.float32(2.0 * math.pi / n)
    return np.cos(theta), np.sin(theta)


def lon_table():
    cos, sin = angles(W, np.arange(KW), np.arange(W))
    both = np.stack([cos, -sin], 1).reshape(G, HL, 2, W)
    full = np.zeros((G, CH * KC, 2, W), np.float32)
    full[:, :HL] = both
    full = full.reshape(G, CH, KC, 2, W).transpose(1, 0, 3, 2, 4)
    return full.reshape(CH, ROWS, W).astype(ml_dtypes.bfloat16)


def lat_table():
    cos, sin = angles(H, np.arange(H), np.arange(H))
    full = np.zeros((G, 2, HP, 2, PP), np.float32)
    cos, sin = cos.reshape(G, HL, H), sin.reshape(G, HL, H)
    full[:, 0, :HL, 0, :H] = cos
    full[:, 1, :HL, 0, :H] = sin
    full[:, 0, :HL, 1, :H] = -sin
    full[:, 1, :HL, 1, :H] = cos
    return full.reshape(G * MSG, 2 * PP).astype(ml_dtypes.bfloat16)


def nt(a, b):
    return lax.dot_general(a, b, (((1,), (1,)), ((), ())), preferred_element_type=F32)


def tn(a, b):
    return lax.dot_general(a, b, (((0,), (0,)), ((), ())), preferred_element_type=F32)


def nn(a, b):
    return jnp.dot(a, b, preferred_element_type=F32)


def kernel(
    x_hbm, y_hbm, lon_hbm, lat_hbm, w1t_ref, w1_ref, w2t_ref, w2_ref, b1_ref, b2_ref,
    out_ref, g_ref,
    x_ref, y_ref, lon_ref, lat_ref, fs, fr, bs, br, work, acc, dy_ref, gw1, gw2, gb1, gb2, gs, gr, hs, hr,
    load_sem, fs_sem, fr_sem, bs_sem, br_sem, gs_sem, gr_sem, hs_sem, hr_sem,
):
    me = lax.axis_index("space")
    row = lax.axis_index("dp")

    barrier = pltpu.get_barrier_semaphore()

    def greet(o, carry):
        pl.semaphore_signal(
            barrier, inc=1, device_id={"space": lax.rem(me + o, G)}, device_id_type=MESH
        )
        pl.semaphore_signal(
            barrier, inc=1, device_id={"dp": lax.rem(row + o, G)}, device_id_type=MESH
        )
        return carry

    lax.fori_loop(1, G, greet, 0)
    loads = [
        pltpu.make_async_copy(src, dst, load_sem.at[i])
        for i, (src, dst) in enumerate(
            [(lon_hbm, lon_ref), (x_hbm, x_ref), (lat_hbm, lat_ref), (y_hbm, y_ref)]
        )
    ]
    for load in loads:
        load.start()
    loads[0].wait()
    loads[1].wait()

    lane = lax.broadcasted_iota(jnp.int32, (HP, CP), 1)

    def longitude(j):
        def two(i, carry):
            pair = x_ref[pl.ds(2 * i, 2)].reshape(2 * CP, W)
            got = nt(lon_ref[j], pair)
            work[pl.ds(pl.multiple_of(2 * i * ROWS, ROWS), ROWS), :] = got[:, :CP]
            work[pl.ds(pl.multiple_of((2 * i + 1) * ROWS, ROWS), ROWS), :] = got[:, CP:]
            return carry

        lax.fori_loop(0, HP // 2, two, 0)

    def packed(owner):
        parts = []
        for half in range(KC // 4):
            rows = []
            for s in range(2):
                a = [
                    work[pl.ds(owner * 2 * KC + s * KC + half * 4 + k, HP, stride=ROWS), :]
                    for k in range(4)
                ]
                r1 = pltpu.roll(a[1], 96, 1)
                r2 = pltpu.roll(a[2], 64, 1)
                r3 = pltpu.roll(a[3], 32, 1)
                rows.append(
                    [
                        jnp.where(lane < 96, a[0], r1),
                        jnp.where(lane < 64, r1, r2),
                        jnp.where(lane < 32, r2, r3),
                    ]
                )
            for t in range(3):
                parts.append(jnp.concatenate([rows[0][t], rows[1][t]], 0).astype(BF16))
        return parts

    def forward_copy(j, peer):
        return pltpu.make_async_remote_copy(
            src_ref=fs.at[j, peer], dst_ref=fr.at[j, me], send_sem=fs_sem.at[j, peer],
            recv_sem=fr_sem.at[j, me], device_id={"space": peer}, device_id_type=MESH,
        )

    def forward_arrival(j, peer):
        return pltpu.make_async_remote_copy(
            src_ref=fs.at[j, peer], dst_ref=fr.at[j, peer], send_sem=fs_sem.at[j, peer],
            recv_sem=fr_sem.at[j, peer], device_id={"space": peer}, device_id_type=MESH,
        )

    def back_copy(j, peer):
        return pltpu.make_async_remote_copy(
            src_ref=bs.at[j, peer], dst_ref=br.at[j, me], send_sem=bs_sem.at[j, peer],
            recv_sem=br_sem.at[j, me], device_id={"space": peer}, device_id_type=MESH,
        )

    def back_arrival(j, peer):
        return pltpu.make_async_remote_copy(
            src_ref=bs.at[j, peer], dst_ref=br.at[j, peer], send_sem=bs_sem.at[j, peer],
            recv_sem=br_sem.at[j, peer], device_id={"space": peer}, device_id_type=MESH,
        )

    def send_chunk(j, carry):
        longitude(j)

        @pl.when(j == 0)
        def _():
            pl.semaphore_wait(barrier, 2 * (G - 1))

        def one(o, c):
            peer = lax.rem(me + o, G)
            for t, part in enumerate(packed(peer)):
                fs[j, peer, :, t * CP : (t + 1) * CP] = part
            forward_copy(j, peer).start()
            return c

        lax.fori_loop(1, G, one, 0)
        for t, part in enumerate(packed(me)):
            fr[j, me, :, t * CP : (t + 1) * CP] = part
        return carry

    lax.fori_loop(0, CH, send_chunk, 0)
    loads[2].wait()
    loads[3].wait()

    gw1[...] = jnp.zeros_like(gw1)
    gw2[...] = jnp.zeros_like(gw2)
    gb1[...] = jnp.zeros_like(gb1)
    gb2[...] = jnp.zeros_like(gb2)

    def folded(v):
        v = v.astype(F32)
        return v[:, :CP] + v[:, CP : 2 * CP] + v[:, 2 * CP :]

    def middle(j, carry):
        def arrive(o, c):
            forward_arrival(j, lax.rem(me + o, G)).wait_recv()
            return c

        lax.fori_loop(1, G, arrive, 0)
        for half in range(KC // 4):
            lanes = slice(half * PP, (half + 1) * PP)
            got = fr[j, :, :, lanes].reshape(G * MSG, PP)
            dz = tn(got, lat_ref[...])
            for k in range(4):
                at = j * KC + half * 4 + k
                mult = jnp.where(at + me == 0, SCALE, 2.0 * SCALE).astype(F32)
                dzk = dz[k * C : (k + 1) * C]
                dzk = jnp.concatenate([dzk[:, :PP], dzk[:, PP:]], 0) * mult
                yk = y_ref[at]
                u = nn(w1t_ref[...], yk) + b1_ref[...]
                a = jnp.maximum(u, 0.0).astype(BF16)
                v = nn(w2t_ref[...], a) + b2_ref[...]
                dv = jnp.where(jnp.abs(v) > LAM, dzk, 0.0).astype(BF16)
                gw2[...] += nt(a, dv)
                gb2[...] += folded(dv)
                da = nn(w2_ref[...], dv)
                du = jnp.where(u > 0.0, da, 0.0).astype(BF16)
                gw1[...] += nt(yk, du)
                gb1[...] += folded(du)
                dy = nn(w1_ref[...], du).astype(BF16)
                dy_ref[k * C : (k + 1) * C, :PP] = dy[:C]
                dy_ref[k * C : (k + 1) * C, PP:] = dy[C:]
            q = nt(lat_ref[...], dy_ref[...]).astype(BF16)
            bs[j, :, :, lanes] = q.reshape(G, MSG, PP)

        def one(o, c):
            back_copy(j, lax.rem(me + o, G)).start()
            return c

        lax.fori_loop(1, G, one, 0)
        br[j, me] = bs[j, me]
        return carry

    lax.fori_loop(0, CH, middle, 0)

    def combined(g):
        re = g[:C, :C] + g[C:, C:]
        im = g[:C, C:] - g[C:, :C]
        return re, im

    sums = []
    for g, b in ((gw1, gb1), (gw2, gb2)):
        total = jnp.sum(b[...], axis=1, keepdims=True)
        for part, bias in zip(combined(g[...]), (total[:C], total[C:])):
            wide = jnp.concatenate([part, jnp.broadcast_to(bias, (C, CP - C))], 1)
            sums.append(wide)
    for d in range(G):
        gs[d] = jnp.concatenate([s[6 * d : 6 * d + 6] for s in sums], 0)

    def grad_copy(peer, at):
        return pltpu.make_async_remote_copy(
            src_ref=gs.at[peer], dst_ref=gr.at[at], send_sem=gs_sem.at[peer],
            recv_sem=gr_sem.at[at], device_id={"dp": peer}, device_id_type=MESH,
        )

    def share_copy(peer, at):
        return pltpu.make_async_remote_copy(
            src_ref=hs, dst_ref=hr.at[at], send_sem=hs_sem.at[peer],
            recv_sem=hr_sem.at[at], device_id={"space": peer}, device_id_type=MESH,
        )

    def over_peers(first, body):
        def step(o, c):
            body(lax.rem(first + o, G))
            return c

        lax.fori_loop(1, G, step, 0)

    over_peers(row, lambda peer: grad_copy(peer, row).start())

    def finish(j):
        over_peers(me, lambda peer: back_arrival(j, peer).wait_recv())

        def unpack(g, c):
            for half in range(KC // 4):
                got = br[j, g, :, half * PP : (half + 1) * PP].astype(F32)
                for s in range(2):
                    p = [got[s * HP : (s + 1) * HP, t * CP : (t + 1) * CP] for t in range(3)]
                    parts = [
                        p[0],
                        jnp.where(lane < 32, pltpu.roll(p[0], 32, 1), pltpu.roll(p[1], 32, 1)),
                        jnp.where(lane < 64, pltpu.roll(p[1], 64, 1), pltpu.roll(p[2], 64, 1)),
                        pltpu.roll(p[2], 96, 1),
                    ]
                    for k in range(4):
                        at = g * 2 * KC + s * KC + half * 4 + k
                        work[pl.ds(at, HP, stride=ROWS), :] = parts[k]
            return c

        lax.fori_loop(0, G, unpack, 0)

        def one(h, c):
            q = work[pl.ds(pl.multiple_of(h * ROWS, ROWS), ROWS), :].astype(BF16)
            new = tn(q, lon_ref[j])[:C]
            if j == 0:
                acc[h] = new
            elif j < CH - 1:
                acc[h] += new
            else:
                total = x_ref[h, :C].astype(F32) + SCALE * (acc[h] + new)
                out_ref[h] = total.astype(BF16)
            return c

        lax.fori_loop(0, HL, one, 0)

    finish(0)
    over_peers(row, lambda peer: grad_copy(peer, peer).wait_recv())
    gr[row] = gs[row]
    hs[...] = jnp.sum(gr[...], axis=0)
    over_peers(me, lambda peer: share_copy(peer, me).start())
    finish(1)
    finish(2)
    over_peers(me, lambda peer: share_copy(peer, peer).wait_recv())
    hr[me] = hs[...]
    g_ref[...] = jnp.sum(hr[...], axis=0)

    for j in range(CH):
        over_peers(me, lambda peer, j=j: forward_copy(j, peer).wait_send())
        over_peers(me, lambda peer, j=j: back_copy(j, peer).wait_send())
    over_peers(row, lambda peer: grad_copy(peer, row).wait_send())
    over_peers(me, lambda peer: share_copy(peer, me).wait_send())


def complex_matrix(w):
    return jnp.concatenate(
        [jnp.concatenate([w[0], w[1]], 1), jnp.concatenate([-w[1], w[0]], 1)], 0
    )


def on_device(cotangent, spectrum, first_weight, first_bias, second_weight, second_bias):
    x = jnp.transpose(cotangent[0], (1, 0, 2))
    x = jnp.pad(x, ((0, HP - HL), (0, CP - C), (0, 0)))
    y = jnp.transpose(spectrum[0], (2, 0, 1, 3)).reshape(HL, 2 * C, H)
    y = jnp.pad(y, ((0, HP - HL), (0, 0), (0, PP - H)))
    w1 = complex_matrix(first_weight[:, 0])
    w2 = complex_matrix(second_weight[:, 0])
    b1 = first_bias.astype(F32).reshape(2 * C, 1)
    b2 = second_bias.astype(F32).reshape(2 * C, 1)
    any_spec = pl.BlockSpec(memory_space=pl.ANY)
    vmem = pl.BlockSpec(memory_space=pltpu.VMEM)
    dma = pltpu.SemaphoreType.DMA
    out, g = pl.pallas_call(
        kernel,
        out_shape=(
            jax.ShapeDtypeStruct((HL, C, W), BF16),
            jax.ShapeDtypeStruct((24, CP), F32),
        ),
        in_specs=[any_spec] * 4 + [vmem] * 6,
        out_specs=(vmem, vmem),
        scratch_shapes=[
            pltpu.VMEM((HP, CP, W), BF16),
            pltpu.VMEM((HP, 2 * C, PP), BF16),
            pltpu.VMEM((CH, ROWS, W), BF16),
            pltpu.VMEM((G * MSG, 2 * PP), BF16),
            pltpu.VMEM((CH, G, MSG, 2 * PP), BF16),
            pltpu.VMEM((CH, G, MSG, 2 * PP), BF16),
            pltpu.VMEM((CH, G, MSG, 2 * PP), BF16),
            pltpu.VMEM((CH, G, MSG, 2 * PP), BF16),
            pltpu.VMEM((HP * ROWS, CP), F32),
            pltpu.VMEM((HL, C, W), F32),
            pltpu.VMEM((4 * C, 2 * PP), BF16),
            pltpu.VMEM((2 * C, 2 * C), F32),
            pltpu.VMEM((2 * C, 2 * C), F32),
            pltpu.VMEM((2 * C, CP), F32),
            pltpu.VMEM((2 * C, CP), F32),
            pltpu.VMEM((G, 24, CP), F32),
            pltpu.VMEM((G, 24, CP), F32),
            pltpu.VMEM((24, CP), F32),
            pltpu.VMEM((G, 24, CP), F32),
            dma((4,)),
            dma((CH, G)),
            dma((CH, G)),
            dma((CH, G)),
            dma((CH, G)),
            dma((G,)),
            dma((G,)),
            dma((G,)),
            dma((G,)),
        ],
        compiler_params=pltpu.CompilerParams(
            collective_id=0, has_side_effects=True, vmem_limit_bytes=60 * 1024 * 1024
        ),
        name="afno_backward",
    )(x, y, jnp.asarray(lon_table()), jnp.asarray(lat_table()), w1.T, w1, w2.T, w2, b1, b2)
    grad_in = jnp.transpose(out, (1, 0, 2))[None]
    parts = g.reshape(4, 6, CP)
    gw = parts[:, :, :C].reshape(2, 2, 1, 6, C)
    gb = parts[:, :, C].reshape(2, 2, 1, 6)
    return (grad_in, gw[0], gb[0], gw[1], gb[1])


def solution(mesh):
    in_specs = (
        P("dp", None, "space", None),
        P("dp", None, None, "space", None),
        P(),
        P(),
        P(),
        P(),
    )
    out_specs = (
        P("dp", None, "space", None),
        P(None, None, "dp", None),
        P(None, None, "dp"),
        P(None, None, "dp", None),
        P(None, None, "dp"),
    )
    return jax.shard_map(
        on_device, mesh=mesh, in_specs=in_specs, out_specs=out_specs, check_vma=False
    )
```

time: 510 us -> 217 us (0.43)
  Pallas kernels: 0 us -> 189 us
  blocking collectives: 178 us -> 0 us
  waiting for transfers between devices: 119 us -> 0 us
  matrix products: 70 us -> 0 us
  local copies, waits for them, and re-layouts: 82.9 us -> 20.6 us
  other arithmetic: 20.9 us -> 2.28 us
  starting transfers between devices: 17.7 us -> 0 us
  between operations: 15.5 us -> 0.66 us
    pallas_call x0 -> x1, Pallas kernels: none -> 189 us  [on_device(): pl.pallas_call(kernel, out_shape=(jax.ShapeDtypeStruct((HL, C, W), BF16),...]
    unnamed x1 -> x0, blocking collectives: 94.9 us -> none
    psum x1 -> x0, blocking collectives: 83.2 us -> none  [on_device(): totals = lax.psum((gw1, gb1, gw2, gb2), 'space')]
    all_to_all x2 -> x0, waiting for transfers between devices: 77.5 us -> none  [the longest x1 77.5 us: on_device(): lax.all_to_all(longitude, 'space', split_axis=2, concat_axis=2, tiled=True)]
    dot_general x34 -> x0, matrix products: 70 us -> none  [the longest x10 46.1 us: contract(): return jnp.einsum(form, left, table, preferred_element_type=jnp.float32)]
    unnamed x2 -> x0, waiting for transfers between devices: 41.7 us -> none
    all_to_all x2 -> x0, starting transfers between devices: 17.6 us -> none  [the longest x1 10.6 us: on_device(): lax.all_to_all(longitude, 'space', split_axis=2, concat_axis=2, tiled=True)]
    another operation x5 -> x0, local copies, waits for them, and re-layouts: 16.4 us -> none  [the longest x3 14.9 us: on_device(): jnp.stack([q_re, q_im]).astype(jnp.bfloat16)]
  transfers between devices with their start and end apart: 3 -> 0, of which waited for: 2 -> 0; matrix products, arithmetic and copies ran while one was open for 5% -> 0% of each run, Pallas kernels for 0% -> 0%
where the time goes in v1:
time: 217 us; the launch traced here: 213 us
  Pallas kernels  189 us (87%)
  local copies, waits for them, and re-layouts  20.6 us (9%)
  other arithmetic  2.28 us (1%)
    pallas_call x1, Pallas kernels, on_device(): pl.pallas_call(kernel, out_shape=(jax.ShapeDtypeStruct((HL, C, W), BF16),...  189 us
    unnamed x5, local copies, waits for them, and re-layouts  5.71 us

profile of v1, /device:TPU:32, one launch (start us, length us, event | category | flops | bytes accessed | tf_op | source)
XLA Modules:
  0.0 213.0 jit_solution(6529150025467847448)
XLA Ops:
  0.6 0.7 fusion
  1.4 0.7 fusion.1
  2.1 0.8 slice_bitcast_fusion.2
  2.9 0.8 slice_bitcast_fusion
  3.6 1.5 reshape.53.b1_ref
  5.1 1.5 reshape.54.b2_ref
  6.6 0.8 maximum_maximum_fusion
  7.4 0.7 copy.19.w1t_ref
  8.1 0.8 copy.20.w2t_ref
  8.8 2.5 %copy.18 = bf16[23,2,96,368]{3,2,1,0:T(8,128)(2,1)S(1)} copy(bf16[23,2,96,368]{3,2,0,1:T(8,128)(2,1)} %bitcast.41) | data formatting | bytes 6500352 | tf_op jit(solution)/shard_map/transpose | solution.py:332
  11.4 0.0 copy-start
  11.4 2.4 %pad.9.y_hbm = bf16[24,192,384]{2,1,0:T(8,128)(2,1)} pad(bf16[23,192,368]{2,1,0:T(8,128)(2,1)S(1)} %bitcast.40, bf16[]{:T(256)} %constant.6.clone.1), padding=0_1x0_0x0_16 | pad | bytes 6789122 | tf_op jit(solution)/shard_map/jit(_pad)/pad | solution.py:333
  13.8 0.6 copy-done
  14.3 2.6 %pad.8.x_hbm = bf16[24,128,768]{2,1,0:T(8,128)(2,1)} pad(bf16[23,96,768]{2,1,0:T(8,128)(2,1)S(1)} %bitcast.43, bf16[]{:T(256)} %constant.6.clone.1), padding=0_1x0_32x0_0 | pad | bytes 8110082 | tf_op jit(solution)/shard_map/jit(_pad)/pad | solution.py:331
  17.0 189.4 %afno_backward.1 = (bf16[23,96,768]{2,1,0:T(8,128)(2,1)}, f32[24,128]{1,0:T(8,128)}) custom-call(bf16[24,128,768]{2,1,0:T(8,128)(2,1)} %pad.8.x_hbm, bf16[24,192,384]{2,1,0:T(8,128)(2,1)} %pad.9.y_hbm, bf16[3,256,768]{2,1,0:T(8,128)(2,1)} %constant.7.clone.lon_hbm, bf16[768,768]{1,0:T(8,128)(2,1)} %constant.8.clone.lat_hbm, bf16[192,192]{1,0:T(8,128)(2,1)} %copy.19.w1t_ref, ...), custom_call_target="tpu_custom_call" | custom-call | tf_op jit(solution)/shard_map/afno_backward/pallas_call | solution.py:341
  206.4 0.7 reshape.48
  207.1 0.7 slice_reduce_fusion
  207.9 0.6 copy.27
  208.5 0.6 copy.25
  209.1 3.9 %copy.34 = bf16[1,96,23,768]{3,1,2,0:T(8,128)(2,1)} copy(bf16[1,96,23,768]{3,1,2,0:T(8,128)(2,1)} %bitcast.42) | data formatting | bytes 6782976
  (1 shorter events, 0.0 us)
Async XLA Ops:
  11.4 3.0 %copy-start = (bf16[1,96,23,768]{3,1,2,0:T(8,128)(2,1)S(1)}, bf16[1,96,23,768]{3,1,2,0:T(8,128)(2,1)}, u32[]{:S(2)}) copy-start(bf16[1,96,23,768]{3,1,2,0:T(8,128)(2,1)} %param.8) | copy-start | bytes 10174468

commit v2 on v1

v2 whole, which is shorter than its diff:
```python
import math

import jax
import jax.numpy as jnp
import ml_dtypes
import numpy as np
from jax import lax
from jax.experimental import pallas as pl
from jax.experimental.pallas import tpu as pltpu
from jax.sharding import PartitionSpec as P

H = 368
W = 768
KW = 368
C = 96
G = 16
HL = 23
HP = 24
CP = 128
KG = 4
ROWS = G * 2 * KG
BASE = (0, 4, 7, 11, 15, 19)
COUNT = (4, 3, 4, 4, 4, 4)
ODD = 1
CHUNKS = ((0,), (1, 2, 3), (4,), (5,))
LANES = (384, 1024, 384, 384)
MOST = 3
MSG = 2 * HP
PP = 384
SCALE = 1.0 / math.sqrt(H * W)
LAM = 0.01
F32 = jnp.float32
BF16 = jnp.bfloat16
MESH = pl.DeviceIdType.MESH


def angles(n, rows, cols):
    index = (rows[:, None].astype(np.int64) * cols[None, :].astype(np.int64)) % n
    theta = index.astype(np.float32) * np.float32(2.0 * math.pi / n)
    return np.cos(theta), np.sin(theta)


def lon_table():
    cos, sin = angles(W, np.arange(KW), np.arange(W))
    both = np.stack([cos, -sin], 1).reshape(G, HL, 2, W).transpose(0, 2, 1, 3)
    full = np.zeros((len(BASE), G, 2, KG, W), np.float32)
    for i, (base, count) in enumerate(zip(BASE, COUNT)):
        full[i, :, :, :count] = both[:, :, base : base + count]
    return full.reshape(len(BASE), ROWS, W).astype(ml_dtypes.bfloat16)


def lat_table():
    cos, sin = angles(H, np.arange(H), np.arange(H))
    full = np.zeros((G, 2, HP, 2, PP), np.float32)
    cos, sin = cos.reshape(G, HL, H), sin.reshape(G, HL, H)
    full[:, 0, :HL, 0, :H] = cos
    full[:, 1, :HL, 0, :H] = sin
    full[:, 0, :HL, 1, :H] = -sin
    full[:, 1, :HL, 1, :H] = cos
    return full.reshape(G * MSG, 2 * PP).astype(ml_dtypes.bfloat16)


def nt(a, b):
    return lax.dot_general(a, b, (((1,), (1,)), ((), ())), preferred_element_type=F32)


def tn(a, b):
    return lax.dot_general(a, b, (((0,), (0,)), ((), ())), preferred_element_type=F32)


def nn(a, b):
    return jnp.dot(a, b, preferred_element_type=F32)


def kernel(
    x_hbm, y_hbm, lon_hbm, lat_hbm, w1_in, b1_in, w2_in, b2_in,
    out_ref, g_ref,
    x_ref, y_ref, lon_ref, lat_ref, fs, fr, bs, br, work, acc, dz_ref, dy_ref, q_ref, rem, pads, few,
    yk_ref, w1t_ref, w1_ref, w2t_ref, w2_ref, b1_ref, b2_ref, gw1, gw2, gb1, gb2, gs, gr, hs, hr,
    load_sem, x_sem, fs_sem, fr_sem, bs_sem, br_sem, gs_sem, gr_sem, hs_sem, hr_sem,
):
    me = lax.axis_index("space")
    row = lax.axis_index("dp")

    barrier = pltpu.get_barrier_semaphore()

    def greet(o, carry):
        pl.semaphore_signal(
            barrier, inc=1, device_id={"space": lax.rem(me + o, G)}, device_id_type=MESH
        )
        pl.semaphore_signal(
            barrier, inc=1, device_id={"dp": lax.rem(row + o, G)}, device_id_type=MESH
        )
        return carry

    lon_first = pltpu.make_async_copy(lon_hbm.at[0], lon_ref.at[0], load_sem.at[0])
    lon_first.start()
    x_loads = []
    for i in range(4):
        part = pl.ds(6 * i, min(6, HL - 6 * i))
        x_loads.append(
            pltpu.make_async_copy(x_hbm.at[part], x_ref.at[part, pl.ds(0, C)], x_sem.at[i])
        )
        x_loads[-1].start()
    lon_rest = pltpu.make_async_copy(
        lon_hbm.at[pl.ds(1, 5)], lon_ref.at[pl.ds(1, 5)], load_sem.at[1]
    )
    lat_load = pltpu.make_async_copy(lat_hbm, lat_ref, load_sem.at[2])
    y_load = pltpu.make_async_copy(y_hbm, y_ref, load_sem.at[3])
    for load in (lon_rest, lat_load, y_load):
        load.start()
    lax.fori_loop(1, G, greet, 0)
    x_ref[:, C:] = jnp.zeros((HP, CP - C, W), BF16)
    x_ref[HL, :C] = jnp.zeros((C, W), BF16)

    lane = lax.broadcasted_iota(jnp.int32, (HP, CP), 1)
    sub = lax.broadcasted_iota(jnp.int32, (HP, CP), 0)
    lane6 = lax.broadcasted_iota(jnp.int32, (6, CP), 1)

    def over_peers(first, body, sign=1):
        def step(o, c):
            body(lax.rem(first + G + sign * o, G))
            return c

        lax.fori_loop(1, G, step, 0)

    def copies(src, dst, send, recv, c):
        def out(peer):
            return pltpu.make_async_remote_copy(
                src_ref=src[c].at[peer], dst_ref=dst[c].at[me], send_sem=send.at[c, peer],
                recv_sem=recv.at[c, me], device_id={"space": peer}, device_id_type=MESH,
            )

        def arrival(peer):
            return pltpu.make_async_remote_copy(
                src_ref=src[c].at[peer], dst_ref=dst[c].at[peer], send_sem=send.at[c, peer],
                recv_sem=recv.at[c, peer], device_id={"space": peer}, device_id_type=MESH,
            )

        return out, arrival

    forward = [copies(fs, fr, fs_sem, fr_sem, c) for c in range(len(CHUNKS))]
    backward = [copies(bs, br, bs_sem, br_sem, c) for c in range(len(CHUNKS))]

    def longitude(groups):
        size = ROWS * len(groups)

        def two(i, carry):
            pair = x_ref[pl.ds(2 * i, 2)].reshape(2 * CP, W)
            table = lon_ref[groups[0] : groups[0] + len(groups)].reshape(size, W)
            got = nt(table, pair)
            work[pl.ds(pl.multiple_of(2 * i * size, ROWS), size), :] = got[:, :CP]
            work[pl.ds(pl.multiple_of((2 * i + 1) * size, ROWS), size), :] = got[:, CP:]
            return carry

        if groups[0] == 0:
            for i in range(4):
                x_loads[i].wait()
                lax.fori_loop(3 * i, 3 * i + 3, two, 0)
        else:
            lax.fori_loop(0, HP // 2, two, 0)

    def quarters(load):
        made = load(0)
        for q in range(1, 4):
            made = jnp.where(lane6 < 32 * q, made, load(q))
        return made

    def padded(tiles, extra, first=0):
        done = []
        for t in range(len(tiles[0])):
            both = []
            for s in range(2):
                v = tiles[s][t]
                if extra is not None and first + t < 6:
                    one = jnp.broadcast_to(extra[s][first + t : first + t + 1], (HP, CP))
                    v = jnp.where(sub == HL, one, v)
                both.append(v)
            done.append(jnp.concatenate(both, 0).astype(BF16))
        return done

    def packed(groups, owner):
        size = ROWS * len(groups)
        tiles, extra = [[], []], None
        for i, group in enumerate(groups):
            for s in range(2):
                at = i * ROWS + owner * 2 * KG + s * KG
                a = [work[pl.ds(at + k, HP, stride=size), :] for k in range(KG)]
                r1 = pltpu.roll(a[1], 96, 1)
                r2 = pltpu.roll(a[2], 64, 1)
                tiles[s].append(jnp.where(lane < 96, a[0], r1))
                tiles[s].append(jnp.where(lane < 64, r1, r2))
                if group == ODD:
                    extra = extra or []
                    extra.append(
                        quarters(
                            lambda q, at=at: pltpu.roll(
                                work[pl.ds(at + 2 + 6 * q * size, 6, stride=size), :],
                                (64 + 32 * q) % CP,
                                1,
                            )
                        )
                    )
                else:
                    tiles[s].append(jnp.where(lane < 32, r2, pltpu.roll(a[3], 32, 1)))
        return padded(tiles, extra)

    for c, groups in enumerate(CHUNKS):
        if c == 0:
            lon_first.wait()
        if c == 1:
            lon_rest.wait()
        longitude(groups)
        if c == 0:
            pl.semaphore_wait(barrier, 2 * (G - 1))

        def send(peer, c=c, groups=groups):
            for t, part in enumerate(packed(groups, peer)):
                fs[c][peer, :, t * CP : (t + 1) * CP] = part
            forward[c][0](peer).start()

        over_peers(me, send)
        for t, part in enumerate(packed(groups, me)):
            fr[c][me, :, t * CP : (t + 1) * CP] = part

    eye = lax.broadcasted_iota(jnp.int32, (C, C), 0) == lax.broadcasted_iota(jnp.int32, (C, C), 1)
    eye = eye.astype(F32).astype(BF16)
    for w, b, m_ref, t_ref, bias_ref in (
        (w1_in, b1_in, w1_ref, w1t_ref, b1_ref),
        (w2_in, b2_in, w2_ref, w2t_ref, b2_ref),
    ):
        wr, wi = w[0].astype(F32), w[1].astype(F32)
        tr, ti = nt(eye, w[0]), nt(eye, w[1])
        m_ref[:C] = jnp.concatenate([wr, wi], 1).astype(BF16)
        m_ref[C:] = jnp.concatenate([-wi, wr], 1).astype(BF16)
        t_ref[:C] = jnp.concatenate([tr, -ti], 1).astype(BF16)
        t_ref[C:] = jnp.concatenate([ti, tr], 1).astype(BF16)
        column = nt(eye, b[...])
        bias_ref[:C] = jnp.broadcast_to(column[:, 0:1], (C, PP))
        bias_ref[C:] = jnp.broadcast_to(column[:, 1:2], (C, PP))
    for ref in (gw1, gw2, gb1, gb2, yk_ref):
        ref[...] = jnp.zeros_like(ref)
    lat_load.wait()
    y_load.wait()

    def folded(v):
        v = v.astype(F32)
        return v[:, :CP] + v[:, CP : 2 * CP] + v[:, 2 * CP :]

    def mix(group):
        def one(k, carry):
            at = BASE[group] + k
            rows = pl.ds(pl.multiple_of(k * C, C), C)
            mult = jnp.where(at + me == 0, SCALE, 2.0 * SCALE).astype(F32)
            dzk = jnp.concatenate([dz_ref[rows, :PP], dz_ref[rows, PP:]], 0) * mult
            yk_ref[:C, :H] = y_ref[0, at]
            yk_ref[C:, :H] = y_ref[1, at]
            yk = yk_ref[...]
            u = nn(w1t_ref[...], yk) + b1_ref[...]
            a = jnp.maximum(u, 0.0).astype(BF16)
            v = nn(w2t_ref[...], a) + b2_ref[...]
            dv = jnp.where(jnp.abs(v) > LAM, dzk, 0.0).astype(BF16)
            gw2[...] += nt(a, dv)
            gb2[...] += folded(dv)
            da = nn(w2_ref[...], dv)
            du = jnp.where(u > 0.0, da, 0.0).astype(BF16)
            gw1[...] += nt(yk, du)
            gb1[...] += folded(du)
            dy = nn(w1_ref[...], du).astype(BF16)
            dy_ref[rows, :PP] = dy[:C]
            dy_ref[rows, PP:] = dy[C:]
            return carry

        lax.fori_loop(0, COUNT[group], one, 0)

    def spread(chunk, g, s, store):
        at = 16 + 16 * s
        v = chunk[g, at : at + 16, : 6 * CP].astype(F32)
        r = HL - 16 if s == 0 else 15
        six = jnp.concatenate([v[r : r + 1, t * CP : (t + 1) * CP] for t in range(6)], 0)
        for q in range(4):
            store(q, six if q == 0 else pltpu.roll(six, CP - 32 * q, 1))

    def middle(c, groups):
        over_peers(me, lambda peer: forward[c][1](peer).wait_recv(), -1)
        if ODD in groups:

            def collect(g, carry):
                for s in range(2):

                    def store(q, v, s=s):
                        rem[pl.ds(g * MSG + s * HP + 6 * q, 6), :] = v

                    spread(fr[c], g, s, store)
                return carry

            lax.fori_loop(0, G, collect, 0)
        lanes = 0
        for group in groups:
            if group == ODD:
                got = fr[c][:, :, : 2 * CP].reshape(G * MSG, 2 * CP)
                got = jnp.concatenate([got, rem[...].astype(BF16)], 1)
            else:
                got = fr[c][:, :, lanes : lanes + PP].reshape(G * MSG, PP)
            dz_ref[...] = tn(got, lat_ref[...])
            mix(group)
            q = nt(lat_ref[...], dy_ref[...])
            width = 2 * CP if group == ODD else PP
            if len(groups) == 1:
                bs[c][...] = q.astype(BF16).reshape(G, MSG, PP)
            else:
                q_ref[...] = q

                def place(g, carry, group=group, lanes=lanes, width=width):
                    tiles, extra = [], []
                    for s in range(2):
                        at = pl.multiple_of(g * MSG + s * HP, 8)
                        v = q_ref[pl.ds(at, HP), :]
                        tiles.append([v[:, t * CP : (t + 1) * CP] for t in range(width // CP)])
                        if group == ODD:

                            def load(q, v=v[:, 2 * CP :]):
                                v = v[6 * q : 6 * q + 6]
                                return v if q == 0 else pltpu.roll(v, 32 * q, 1)

                            pads[g, s, :6] = quarters(load)
                        extra.append(pads[g, s])
                    for t, part in enumerate(padded(tiles, extra, lanes // CP)):
                        bs[c][g, :, lanes + t * CP : lanes + (t + 1) * CP] = part
                    return carry

                lax.fori_loop(0, G, place, 0)
            lanes += width

    def send_back(c):
        over_peers(me, lambda peer: backward[c][0](peer).start())
        br[c][me] = bs[c][me]

    for c in range(3):
        middle(c, CHUNKS[c])
        send_back(c)
    middle(3, CHUNKS[3])

    def combined(g):
        re = g[:C, :C] + g[C:, C:]
        im = g[:C, C:] - g[C:, :C]
        return re, im

    sums = []
    for g, b in ((gw1, gb1), (gw2, gb2)):
        total = jnp.sum(b[...], axis=1, keepdims=True)
        for part, bias in zip(combined(g[...]), (total[:C], total[C:])):
            wide = jnp.concatenate([part, jnp.broadcast_to(bias, (C, CP - C))], 1)
            sums.append(wide)
    for d in range(G):
        gs[d] = jnp.concatenate([s[6 * d : 6 * d + 6] for s in sums], 0)

    def grad_copy(peer, at):
        return pltpu.make_async_remote_copy(
            src_ref=gs.at[peer], dst_ref=gr.at[at], send_sem=gs_sem.at[peer],
            recv_sem=gr_sem.at[at], device_id={"dp": peer}, device_id_type=MESH,
        )

    def share_copy(peer, at):
        return pltpu.make_async_remote_copy(
            src_ref=hs, dst_ref=hr.at[at], send_sem=hs_sem.at[peer],
            recv_sem=hr_sem.at[at], device_id={"space": peer}, device_id_type=MESH,
        )

    over_peers(row, lambda peer: grad_copy(peer, row).start())
    send_back(3)

    def finish(c, groups):
        size = ROWS * len(groups)

        def unpack(g):
            lanes = 0
            for i, group in enumerate(groups):
                width = 2 * CP if group == ODD else PP
                got = br[c][g, :, lanes : lanes + width].astype(F32)
                for s in range(2):
                    p = [
                        got[s * HP : (s + 1) * HP, t * CP : (t + 1) * CP]
                        for t in range(width // CP)
                    ]
                    parts = [
                        p[0],
                        jnp.where(lane < 32, pltpu.roll(p[0], 32, 1), pltpu.roll(p[1], 32, 1)),
                    ]
                    if group == ODD:

                        def store(q, v, s=s):
                            few[s, 6 * q : 6 * q + 6, :] = v

                        spread(br[c], g, s, store)
                        last = few[s]
                    else:
                        last = p[2]
                    parts.append(
                        jnp.where(lane < 64, pltpu.roll(p[1], 64, 1), pltpu.roll(last, 64, 1))
                    )
                    if group == ODD:
                        parts.append(jnp.zeros((HP, CP), F32))
                    else:
                        parts.append(pltpu.roll(last, 96, 1))
                    for k in range(KG):
                        at = i * ROWS + g * 2 * KG + s * KG + k
                        work[pl.ds(at, HP, stride=size), :] = parts[k]
                lanes += width

        unpack(me)

        def step(peer):
            backward[c][1](peer).wait_recv()
            unpack(peer)

        over_peers(me, step, -1)
        table = lon_ref[groups[0] : groups[0] + len(groups)].reshape(size, W)

        def block(first, count):
            columns = []
            for i in range(count):
                v = work[pl.ds(pl.multiple_of((first + i) * size, ROWS), size), :].astype(BF16)
                columns.append(jnp.transpose(v)[:C])
            new = nn(jnp.concatenate(columns, 0), table).reshape(count, C, W) * SCALE
            at = pl.ds(first, count)
            if c == 0:
                acc[at] = x_ref[at, :C].astype(F32) + new
            elif c < len(CHUNKS) - 1:
                acc[at] += new
            else:
                out_ref[at] = (acc[at] + new).astype(BF16)

        def four(i, carry):
            block(4 * i, 4)
            return carry

        lax.fori_loop(0, HL // 4, four, 0)
        block(HL // 4 * 4, HL % 4)

    for c in range(3):
        finish(c, CHUNKS[c])
    over_peers(row, lambda peer: grad_copy(peer, peer).wait_recv(), -1)
    gr[row] = gs[row]
    hs[...] = jnp.sum(gr[...], axis=0)
    over_peers(me, lambda peer: share_copy(peer, me).start())
    finish(3, CHUNKS[3])
    over_peers(me, lambda peer: share_copy(peer, peer).wait_recv(), -1)
    hr[me] = hs[...]
    total = jnp.sum(hr[...], axis=0)
    for i in range(4):
        g_ref[i] = total[6 * i : 6 * i + 6]

    for c in range(len(CHUNKS)):
        over_peers(me, lambda peer, c=c: forward[c][0](peer).wait_send())
        over_peers(me, lambda peer, c=c: backward[c][0](peer).wait_send())
    over_peers(row, lambda peer: grad_copy(peer, row).wait_send())
    over_peers(me, lambda peer: share_copy(peer, me).wait_send())


def on_device(cotangent, spectrum, first_weight, first_bias, second_weight, second_bias):
    x = jnp.transpose(cotangent[0], (1, 0, 2))
    y = jnp.transpose(spectrum[0], (0, 2, 1, 3))
    any_spec = pl.BlockSpec(memory_space=pl.ANY)
    vmem = pl.BlockSpec(memory_space=pltpu.VMEM)
    dma = pltpu.SemaphoreType.DMA
    messages = [pltpu.VMEM((G, MSG, lanes), BF16) for lanes in LANES]
    n = len(CHUNKS)
    out, g = pl.pallas_call(
        kernel,
        out_shape=(
            pltpu.VMEM((HL, C, W), BF16),
            jax.ShapeDtypeStruct((4, 6, CP), F32),
        ),
        in_specs=[any_spec] * 4 + [vmem] * 4,
        out_specs=(vmem, vmem),
        scratch_shapes=[
            pltpu.VMEM((HP, CP, W), BF16),
            pltpu.VMEM((2, HL, C, H), BF16),
            pltpu.VMEM((len(BASE), ROWS, W), BF16),
            pltpu.VMEM((G * MSG, 2 * PP), BF16),
            messages,
            messages,
            messages,
            messages,
            pltpu.VMEM((HP * MOST * ROWS, CP), F32),
            pltpu.VMEM((HL, C, W), F32),
            pltpu.VMEM((KG * C, 2 * PP), F32),
            pltpu.VMEM((KG * C, 2 * PP), BF16),
            pltpu.VMEM((G * MSG, PP), F32),
            pltpu.VMEM((G * MSG, CP), F32),
            pltpu.VMEM((G, 2, 8, CP), F32),
            pltpu.VMEM((2, HP, CP), F32),
            pltpu.VMEM((2 * C, PP), BF16),
            pltpu.VMEM((2 * C, 2 * C), BF16),
            pltpu.VMEM((2 * C, 2 * C), BF16),
            pltpu.VMEM((2 * C, 2 * C), BF16),
            pltpu.VMEM((2 * C, 2 * C), BF16),
            pltpu.VMEM((2 * C, PP), F32),
            pltpu.VMEM((2 * C, PP), F32),
            pltpu.VMEM((2 * C, 2 * C), F32),
            pltpu.VMEM((2 * C, 2 * C), F32),
            pltpu.VMEM((2 * C, CP), F32),
            pltpu.VMEM((2 * C, CP), F32),
            pltpu.VMEM((G, 24, CP), F32),
            pltpu.VMEM((G, 24, CP), F32),
            pltpu.VMEM((24, CP), F32),
            pltpu.VMEM((G, 24, CP), F32),
            dma((4,)),
            dma((4,)),
            dma((n, G)),
            dma((n, G)),
            dma((n, G)),
            dma((n, G)),
            dma((G,)),
            dma((G,)),
            dma((G,)),
            dma((G,)),
        ],
        compiler_params=pltpu.CompilerParams(
            collective_id=0, has_side_effects=True, vmem_limit_bytes=52 * 1024 * 1024
        ),
        name="afno_backward",
    )(
        x, y, jnp.asarray(lon_table()), jnp.asarray(lat_table()),
        first_weight[:, 0], first_bias[:, 0], second_weight[:, 0], second_bias[:, 0],
    )
    grad_in = jnp.transpose(out, (1, 0, 2))[None]
    gw = g[:, :, :C].reshape(2, 2, 1, 6, C)
    gb = g[:, :, C].reshape(2, 2, 1, 6)
    return (grad_in, gw[0], gb[0], gw[1], gb[1])


def solution(mesh):
    in_specs = (
        P("dp", None, "space", None),
        P("dp", None, None, "space", None),
        P(),
        P(),
        P(),
        P(),
    )
    out_specs = (
        P("dp", None, "space", None),
        P(None, None, "dp", None),
        P(None, None, "dp"),
        P(None, None, "dp", None),
        P(None, None, "dp"),
    )
    return jax.shard_map(
        on_device, mesh=mesh, in_specs=in_specs, out_specs=out_specs, check_vma=False
    )
```

time: 217 us -> 175 us (0.81); the launches traced: 213 us -> 175 us
  Pallas kernels: 189 us -> 169 us
  local copies, waits for them, and re-layouts: 20.6 us -> 5.09 us
  other arithmetic: 2.28 us -> 0 us
    pallas_call x1, Pallas kernels: 189 us -> 169 us  [on_device(): pl.pallas_call(kernel, out_shape=(pltpu.VMEM((HL, C, W), BF16), jax.Shape...]
    pad x2 -> x0, local copies, waits for them, and re-layouts: 5.01 us -> none  [the longest x1 2.65 us: on_device(): x = jnp.pad(x, ((0, HP - HL), (0, CP - C), (0, 0)))]
    transpose x3 -> x0, local copies, waits for them, and re-layouts: 4.02 us -> none  [the longest x1 2.52 us: on_device(): y = jnp.transpose(spectrum[0], (2, 0, 1, 3)).reshape(HL, 2 * C, H)]
    reshape x3 -> x0, local copies, waits for them, and re-layouts: 3.63 us -> none  [the longest x1 1.46 us: on_device(): b2 = second_bias.astype(F32).reshape(2 * C, 1)]
    unnamed x5 -> x3, local copies, waits for them, and re-layouts: 5.71 us -> 2.95 us
where the time goes in v2:
time: 175 us
  Pallas kernels  169 us (97%)
  local copies, waits for them, and re-layouts  5.09 us (3%)
    pallas_call x1, Pallas kernels, on_device(): pl.pallas_call(kernel, out_shape=(pltpu.VMEM((HL, C, W), BF16), jax.Shape...  169 us

profile of v2, /device:TPU:32, one launch (start us, length us, event | category | flops | bytes accessed | tf_op | source)
XLA Modules:
  0.0 174.8 jit_solution(9687338277965334548)
XLA Ops:
  0.6 169.0 %afno_backward.1 = (bf16[23,96,768]{2,1,0:T(8,128)(2,1)S(1)}, f32[4,6,128]{2,1,0:T(8,128)}) custom-call(bf16[23,96,768]{2,1,0:T(8,128)(2,1)} %bitcast.24, bf16[2,23,96,368]{3,2,1,0:T(8,128)(2,1)} %bitcast.25, bf16[6,128,768]{2,1,0:T(8,128)(2,1)} %constant.4.clone.lon_hbm, bf16[768,768]{1,0:T(8,128)(2,1)} %constant.5.clone.lat_hbm, ...), custom_call_target="tpu_custom_call" | custom-call | tf_op jit(solution)/shard_map/afno_backward/pallas_call | solution.py:469
  169.7 0.7 slice_bitcast_fusion
  170.4 0.6 copy.17
  171.0 0.6 copy.19
  171.6 1.4 slice_reduce_fusion
  173.0 1.7 copy.22

commit v3 on v2

--- a/solution.py
+++ b/solution.py
@@ -73,24 +73,45 @@
 
 
 def kernel(
-    x_hbm, y_hbm, lon_hbm, lat_hbm, w1_in, b1_in, w2_in, b2_in,
+    x_hbm, y_hbm, lon_hbm, lat_hbm, w1_hbm, b1_hbm, w2_hbm, b2_hbm,
     out_ref, g_ref,
-    x_ref, y_ref, lon_ref, lat_ref, fs, fr, bs, br, work, acc, dz_ref, dy_ref, q_ref, rem, pads, few,
-    yk_ref, w1t_ref, w1_ref, w2t_ref, w2_ref, b1_ref, b2_ref, gw1, gw2, gb1, gb2, gs, gr, hs, hr,
-    load_sem, x_sem, fs_sem, fr_sem, bs_sem, br_sem, gs_sem, gr_sem, hs_sem, hr_sem,
+    w1_in, b1_in, w2_in, b2_in, x_ref, y_ref, lon_ref, lat_ref, fs, fr, bs, br, work, acc, dz_ref, dy_ref, q_ref, rem, pads, few,
+    yk_ref, w1t_ref, w1_ref, w2t_ref, w2_ref, b1_ref, b2_ref, gw1, gw2, gb1, gb2,
+    gs, gr, hs, hr, zs, zr, ts, tr,
+    load_sem, small_sem, x_sem, fs_sem, fr_sem, bs_sem, br_sem,
+    gs_sem, gr_sem, hs_sem, hr_sem, zs_sem, zr_sem, ts_sem, tr_sem,
 ):
     me = lax.axis_index("space")
     row = lax.axis_index("dp")
 
+    my_x, my_zh = me // 4, lax.rem(me, 4)
+    my_zl, my_yc = row // 8, lax.rem(row, 8)
+
+    def yc_peer(yc):
+        return {"dp": my_zl * 8 + yc}
+
+    def x_peer(x):
+        return {"space": x * 4 + my_zh}
+
+    def z_peer(z):
+        return {"dp": (z // 4) * 8 + my_yc, "space": my_x * 4 + lax.rem(z, 4)}
+
+    my_z = my_zl * 4 + my_zh
     barrier = pltpu.get_barrier_semaphore()
 
-    def greet(o, carry):
-        pl.semaphore_signal(
-            barrier, inc=1, device_id={"space": lax.rem(me + o, G)}, device_id_type=MESH
-        )
-        pl.semaphore_signal(
-            barrier, inc=1, device_id={"dp": lax.rem(row + o, G)}, device_id_type=MESH
-        )
+    def greet(device):
+        pl.semaphore_signal(barrier, inc=1, device_id=device, device_id_type=MESH)
+
+    def greet_space(o, carry):
+        greet({"space": lax.rem(me + o, G)})
+        return carry
+
+    def greet_yc(o, carry):
+        greet(yc_peer(lax.rem(my_yc + o, 8)))
+        return carry
+
+    def greet_z(o, carry):
+        greet(z_peer((1 - my_zl) * 4 + o))
         return carry
 
     lon_first = pltpu.make_async_copy(lon_hbm.at[0], lon_ref.at[0], load_sem.at[0])
@@ -107,9 +128,15 @@
     )
     lat_load = pltpu.make_async_copy(lat_hbm, lat_ref, load_sem.at[2])
     y_load = pltpu.make_async_copy(y_hbm, y_ref, load_sem.at[3])
-    for load in (lon_rest, lat_load, y_load):
-        load.start()
-    lax.fori_loop(1, G, greet, 0)
+    small = [
+        pltpu.make_async_copy(src, dst, small_sem.at[i])
+        for i, (src, dst) in enumerate(
+            [(w1_hbm, w1_in), (b1_hbm, b1_in), (w2_hbm, w2_in), (b2_hbm, b2_in)]
+        )
+    ]
+    lax.fori_loop(1, G, greet_space, 0)
+    lax.fori_loop(1, 8, greet_yc, 0)
+    lax.fori_loop(0, 4, greet_z, 0)
     x_ref[:, C:] = jnp.zeros((HP, CP - C, W), BF16)
     x_ref[HL, :C] = jnp.zeros((C, W), BF16)
 
@@ -117,12 +144,12 @@
     sub = lax.broadcasted_iota(jnp.int32, (HP, CP), 0)
     lane6 = lax.broadcasted_iota(jnp.int32, (6, CP), 1)
 
-    def over_peers(first, body, sign=1):
+    def over_peers(first, body, sign=1, n=G):
         def step(o, c):
-            body(lax.rem(first + G + sign * o, G))
+            body(lax.rem(first + n + sign * o, n))
             return c
 
-        lax.fori_loop(1, G, step, 0)
+        lax.fori_loop(1, n, step, 0)
 
     def copies(src, dst, send, recv, c):
         def out(peer):
@@ -156,6 +183,9 @@
         if groups[0] == 0:
             for i in range(4):
                 x_loads[i].wait()
+                if i == 3:
+                    for load in (lon_rest, lat_load, y_load, *small):
+                        load.start()
                 lax.fori_loop(3 * i, 3 * i + 3, two, 0)
         else:
             lax.fori_loop(0, HP // 2, two, 0)
@@ -212,17 +242,26 @@
             lon_rest.wait()
         longitude(groups)
         if c == 0:
-            pl.semaphore_wait(barrier, 2 * (G - 1))
-
-        def send(peer, c=c, groups=groups):
-            for t, part in enumerate(packed(groups, peer)):
-                fs[c][peer, :, t * CP : (t + 1) * CP] = part
-            forward[c][0](peer).start()
-
-        over_peers(me, send)
+            pl.semaphore_wait(barrier, 15 + 7 + 4)
+
+        def send(peers, c=c, groups=groups):
+            for peer in peers:
+                for t, part in enumerate(packed(groups, peer)):
+                    fs[c][peer, :, t * CP : (t + 1) * CP] = part
+            for peer in peers:
+                forward[c][0](peer).start()
+
+        def send_two(i, carry, send=send):
+            send([lax.rem(me + 2 * i, G), lax.rem(me + 2 * i + 1, G)])
+            return carry
+
+        send([lax.rem(me + 1, G)])
+        lax.fori_loop(1, G // 2, send_two, 0)
         for t, part in enumerate(packed(groups, me)):
             fr[c][me, :, t * CP : (t + 1) * CP] = part
 
+    for load in (lat_load, y_load, *small):
+        load.wait()
     eye = lax.broadcasted_iota(jnp.int32, (C, C), 0) == lax.broadcasted_iota(jnp.int32, (C, C), 1)
     eye = eye.astype(F32).astype(BF16)
     for w, b, m_ref, t_ref, bias_ref in (
@@ -230,32 +269,30 @@
         (w2_in, b2_in, w2_ref, w2t_ref, b2_ref),
     ):
         wr, wi = w[0].astype(F32), w[1].astype(F32)
-        tr, ti = nt(eye, w[0]), nt(eye, w[1])
+        wrt, wit = nt(eye, w[0]), nt(eye, w[1])
         m_ref[:C] = jnp.concatenate([wr, wi], 1).astype(BF16)
         m_ref[C:] = jnp.concatenate([-wi, wr], 1).astype(BF16)
-        t_ref[:C] = jnp.concatenate([tr, -ti], 1).astype(BF16)
-        t_ref[C:] = jnp.concatenate([ti, tr], 1).astype(BF16)
+        t_ref[:C] = jnp.concatenate([wrt, -wit], 1).astype(BF16)
+        t_ref[C:] = jnp.concatenate([wit, wrt], 1).astype(BF16)
         column = nt(eye, b[...])
         bias_ref[:C] = jnp.broadcast_to(column[:, 0:1], (C, PP))
         bias_ref[C:] = jnp.broadcast_to(column[:, 1:2], (C, PP))
     for ref in (gw1, gw2, gb1, gb2, yk_ref):
         ref[...] = jnp.zeros_like(ref)
-    lat_load.wait()
-    y_load.wait()
 
     def folded(v):
         v = v.astype(F32)
         return v[:, :CP] + v[:, CP : 2 * CP] + v[:, 2 * CP :]
 
     def mix(group):
-        def one(k, carry):
+        for k in range(COUNT[group]):
             at = BASE[group] + k
-            rows = pl.ds(pl.multiple_of(k * C, C), C)
+            rows = slice(k * C, (k + 1) * C)
             mult = jnp.where(at + me == 0, SCALE, 2.0 * SCALE).astype(F32)
             dzk = jnp.concatenate([dz_ref[rows, :PP], dz_ref[rows, PP:]], 0) * mult
-            yk_ref[:C, :H] = y_ref[0, at]
-            yk_ref[C:, :H] = y_ref[1, at]
-            yk = yk_ref[...]
+            yk_ref[k, :C, :H] = y_ref[0, at]
+            yk_ref[k, C:, :H] = y_ref[1, at]
+            yk = yk_ref[k]
             u = nn(w1t_ref[...], yk) + b1_ref[...]
             a = jnp.maximum(u, 0.0).astype(BF16)
             v = nn(w2t_ref[...], a) + b2_ref[...]
@@ -269,9 +306,6 @@
             dy = nn(w1_ref[...], du).astype(BF16)
             dy_ref[rows, :PP] = dy[:C]
             dy_ref[rows, PP:] = dy[C:]
-            return carry
-
-        lax.fori_loop(0, COUNT[group], one, 0)
 
     def spread(chunk, g, s, store):
         at = 16 + 16 * s
@@ -352,22 +386,47 @@
         for part, bias in zip(combined(g[...]), (total[:C], total[C:])):
             wide = jnp.concatenate([part, jnp.broadcast_to(bias, (C, CP - C))], 1)
             sums.append(wide)
+    zero2 = jnp.zeros((2, CP), F32)
     for d in range(G):
-        gs[d] = jnp.concatenate([s[6 * d : 6 * d + 6] for s in sums], 0)
-
-    def grad_copy(peer, at):
+        for i, v in enumerate(sums):
+            gs[d % 8, d // 8, 8 * i : 8 * i + 8] = jnp.concatenate([v[6 * d : 6 * d + 6], zero2], 0)
+
+    def yc_copy(peer, at):
         return pltpu.make_async_remote_copy(
             src_ref=gs.at[peer], dst_ref=gr.at[at], send_sem=gs_sem.at[peer],
-            recv_sem=gr_sem.at[at], device_id={"dp": peer}, device_id_type=MESH,
+            recv_sem=gr_sem.at[at], device_id=yc_peer(peer), device_id_type=MESH,
+        )
+
+    def x_copy(peer, at):
+        return pltpu.make_async_remote_copy(
+            src_ref=hs.at[peer], dst_ref=hr.at[at], send_sem=hs_sem.at[peer],
+            recv_sem=hr_sem.at[at], device_id=x_peer(peer), device_id_type=MESH,
+        )
+
+    def z_copy(peer, at):
+        return pltpu.make_async_remote_copy(
+            src_ref=zs.at[peer // 4], dst_ref=zr.at[at], send_sem=zs_sem.at[peer],
+            recv_sem=zr_sem.at[at], device_id=z_peer(peer), device_id_type=MESH,
         )
 
     def share_copy(peer, at):
         return pltpu.make_async_remote_copy(
-            src_ref=hs, dst_ref=hr.at[at], send_sem=hs_sem.at[peer],
-            recv_sem=hr_sem.at[at], device_id={"space": peer}, device_id_type=MESH,
+            src_ref=ts, dst_ref=tr.at[at], send_sem=ts_sem.at[peer],
+            recv_sem=tr_sem.at[at], device_id=x_peer(peer), device_id_type=MESH,
         )
 
-    over_peers(row, lambda peer: grad_copy(peer, row).start())
+    over_peers(my_yc, lambda peer: yc_copy(peer, my_yc).start(), 1, 8)
+    gr[my_yc] = gs[my_yc]
+    over_peers(my_yc, lambda peer: yc_copy(peer, peer).wait_recv(), -1, 8)
+    total = jnp.sum(gr[...], axis=0)
+    for x in range(4):
+        hs[x] = total[:, 8 * x : 8 * x + 8]
+    over_peers(my_x, lambda peer: x_copy(peer, my_x).start(), 1, 4)
+    hr[my_x] = hs[my_x]
+    over_peers(my_x, lambda peer: x_copy(peer, peer).wait_recv(), -1, 4)
+    zs[...] = jnp.sum(hr[...], axis=0)
+    over_peers(my_z, lambda peer: z_copy(peer, my_z).start(), 1, 8)
+    zr[my_z] = zs[my_zl]
     send_back(3)
 
     def finish(c, groups):
@@ -408,13 +467,22 @@
                         work[pl.ds(at, HP, stride=size), :] = parts[k]
                 lanes += width
 
+        def arrived(peers):
+            for peer in peers:
+                backward[c][1](peer).wait_recv()
+
+        def two(i, carry):
+            peers = [lax.rem(me + G - 2 * i, G), lax.rem(me + G - 2 * i - 1, G)]
+            arrived(peers)
+            for peer in peers:
+                unpack(peer)
+            return carry
+
+        first = lax.rem(me + G - 1, G)
+        arrived([first])
         unpack(me)
-
-        def step(peer):
-            backward[c][1](peer).wait_recv()
-            unpack(peer)
-
-        over_peers(me, step, -1)
+        unpack(first)
+        lax.fori_loop(1, G // 2, two, 0)
         table = lon_ref[groups[0] : groups[0] + len(groups)].reshape(size, W)
 
         def block(first, count):
@@ -438,24 +506,35 @@
         lax.fori_loop(0, HL // 4, four, 0)
         block(HL // 4 * 4, HL % 4)
 
+    for c in range(len(CHUNKS)):
+        over_peers(me, lambda peer, c=c: forward[c][0](peer).wait_send())
+    over_peers(my_yc, lambda peer: yc_copy(peer, my_yc).wait_send(), 1, 8)
+    over_peers(my_x, lambda peer: x_copy(peer, my_x).wait_send(), 1, 4)
     for c in range(3):
         finish(c, CHUNKS[c])
-    over_peers(row, lambda peer: grad_copy(peer, peer).wait_recv(), -1)
-    gr[row] = gs[row]
-    hs[...] = jnp.sum(gr[...], axis=0)
-    over_peers(me, lambda peer: share_copy(peer, me).start())
+        over_peers(me, lambda peer, c=c: backward[c][0](peer).wait_send())
+    over_peers(my_z, lambda peer: z_copy(peer, my_z).wait_send(), 1, 8)
+    over_peers(my_z, lambda peer: z_copy(peer, peer).wait_recv(), -1, 8)
+    ts[...] = jnp.sum(zr[...], axis=0)
+    over_peers(my_x, lambda peer: share_copy(peer, my_x).start(), 1, 4)
+    tr[my_x] = ts[...]
     finish(3, CHUNKS[3])
-    over_peers(me, lambda peer: share_copy(peer, peer).wait_recv(), -1)
-    hr[me] = hs[...]
-    total = jnp.sum(hr[...], axis=0)
-    for i in range(4):
-        g_ref[i] = total[6 * i : 6 * i + 6]
-
-    for c in range(len(CHUNKS)):
-        over_peers(me, lambda peer, c=c: forward[c][0](peer).wait_send())
-        over_peers(me, lambda peer, c=c: backward[c][0](peer).wait_send())
-    over_peers(row, lambda peer: grad_copy(peer, row).wait_send())
-    over_peers(me, lambda peer: share_copy(peer, me).wait_send())
+    over_peers(my_x, lambda peer: share_copy(peer, peer).wait_recv(), -1, 4)
+    g_ref[...] = tr[...]
+    over_peers(me, lambda peer: backward[3][0](peer).wait_send())
+    over_peers(my_x, lambda peer: share_copy(peer, my_x).wait_send(), 1, 4)
+
+
+def emit(g_in, gw1_ref, gb1_ref, gw2_ref, gb2_ref):
+    rows = lax.broadcasted_iota(jnp.int32, (8, CP), 0)
+    lanes = lax.broadcasted_iota(jnp.int32, (8, CP), 1)
+    for i, (w_ref, b_ref) in enumerate(((gw1_ref, gb1_ref), (gw2_ref, gb2_ref))):
+        for s in range(2):
+            v = g_in[2 * i + s]
+            for r in range(6):
+                w_ref[s, r, :, :] = v[r : r + 1, :C]
+            spread = jnp.where(rows == lanes, jnp.broadcast_to(v[:, C : C + 1], (8, CP)), 0.0)
+            b_ref[s, :, :] = jnp.sum(spread, axis=0, keepdims=True)[:, :6]
 
 
 def on_device(cotangent, spectrum, first_weight, first_bias, second_weight, second_bias):
@@ -470,11 +549,15 @@
         kernel,
         out_shape=(
             pltpu.VMEM((HL, C, W), BF16),
-            jax.ShapeDtypeStruct((4, 6, CP), F32),
+            pltpu.VMEM((4, 8, CP), F32),
         ),
-        in_specs=[any_spec] * 4 + [vmem] * 4,
+        in_specs=[any_spec] * 8,
         out_specs=(vmem, vmem),
         scratch_shapes=[
+            pltpu.VMEM((2, C, C), BF16),
+            pltpu.VMEM((2, C), BF16),
+            pltpu.VMEM((2, C, C), BF16),
+            pltpu.VMEM((2, C), BF16),
             pltpu.VMEM((HP, CP, W), BF16),
             pltpu.VMEM((2, HL, C, H), BF16),
             pltpu.VMEM((len(BASE), ROWS, W), BF16),
@@ -491,7 +574,7 @@
             pltpu.VMEM((G * MSG, CP), F32),
             pltpu.VMEM((G, 2, 8, CP), F32),
             pltpu.VMEM((2, HP, CP), F32),
-            pltpu.VMEM((2 * C, PP), BF16),
+            pltpu.VMEM((KG, 2 * C, PP), BF16),
             pltpu.VMEM((2 * C, 2 * C), BF16),
             pltpu.VMEM((2 * C, 2 * C), BF16),
             pltpu.VMEM((2 * C, 2 * C), BF16),
@@ -502,20 +585,29 @@
             pltpu.VMEM((2 * C, 2 * C), F32),
             pltpu.VMEM((2 * C, CP), F32),
             pltpu.VMEM((2 * C, CP), F32),
-            pltpu.VMEM((G, 24, CP), F32),
-            pltpu.VMEM((G, 24, CP), F32),
-            pltpu.VMEM((24, CP), F32),
-            pltpu.VMEM((G, 24, CP), F32),
+            pltpu.VMEM((8, 2, 32, CP), F32),
+            pltpu.VMEM((8, 2, 32, CP), F32),
+            pltpu.VMEM((4, 2, 8, CP), F32),
+            pltpu.VMEM((4, 2, 8, CP), F32),
+            pltpu.VMEM((2, 8, CP), F32),
+            pltpu.VMEM((8, 8, CP), F32),
+            pltpu.VMEM((8, CP), F32),
+            pltpu.VMEM((4, 8, CP), F32),
+            dma((4,)),
             dma((4,)),
             dma((4,)),
             dma((n, G)),
             dma((n, G)),
             dma((n, G)),
             dma((n, G)),
-            dma((G,)),
-            dma((G,)),
-            dma((G,)),
-            dma((G,)),
+            dma((8,)),
+            dma((8,)),
+            dma((4,)),
+            dma((4,)),
+            dma((8,)),
+            dma((8,)),
+            dma((4,)),
+            dma((4,)),
         ],
         compiler_params=pltpu.CompilerParams(
             collective_id=0, has_side_effects=True, vmem_limit_bytes=52 * 1024 * 1024
@@ -525,10 +617,21 @@
         x, y, jnp.asarray(lon_table()), jnp.asarray(lat_table()),
         first_weight[:, 0], first_bias[:, 0], second_weight[:, 0], second_bias[:, 0],
     )
+    gw1, gb1, gw2, gb2 = pl.pallas_call(
+        emit,
+        out_shape=(
+            jax.ShapeDtypeStruct((2, 6, 1, C), F32),
+            jax.ShapeDtypeStruct((2, 1, 6), F32),
+            jax.ShapeDtypeStruct((2, 6, 1, C), F32),
+            jax.ShapeDtypeStruct((2, 1, 6), F32),
+        ),
+        in_specs=[vmem],
+        out_specs=(vmem, vmem, vmem, vmem),
+        name="emit",
+    )(pltpu.with_memory_space_constraint(g, pltpu.VMEM))
     grad_in = jnp.transpose(out, (1, 0, 2))[None]
-    gw = g[:, :, :C].reshape(2, 2, 1, 6, C)
-    gb = g[:, :, C].reshape(2, 2, 1, 6)
-    return (grad_in, gw[0], gb[0], gw[1], gb[1])
+    gw1, gw2 = [jnp.transpose(v, (0, 2, 1, 3)) for v in (gw1, gw2)]
+    return (grad_in, gw1, gb1, gw2, gb2)
 
 
 def solution(mesh):

time: 175 us -> 169 us (0.966)
  local copies, waits for them, and re-layouts: 5.09 us -> 1.74 us
  Pallas kernels: 169 us -> 166 us
    pallas_call x1 -> x2, Pallas kernels: 169 us -> 166 us  [the longest x1 166 us: on_device(): pl.pallas_call(kernel, out_shape=(pltpu.VMEM((HL, C, W), BF16), pltpu.VME...]
where the time goes in v3:
time: 169 us
  Pallas kernels  166 us (98%)
  local copies, waits for them, and re-layouts  1.74 us (1%)
    pallas_call x1, Pallas kernels, on_device(): pl.pallas_call(kernel, out_shape=(pltpu.VMEM((HL, C, W), BF16), pltpu.VME...  166 us

profile of v3, /device:TPU:32, one launch (start us, length us, event | category | flops | bytes accessed | tf_op | source)
XLA Modules:
  0.0 168.7 jit_solution(523989678369360349)
XLA Ops:
  0.6 165.6 %afno_backward.1 = (bf16[23,96,768]{2,1,0:T(8,128)(2,1)S(1)}, f32[4,8,128]{2,1,0:T(8,128)S(1)}) custom-call(bf16[23,96,768]{2,1,0:T(8,128)(2,1)} %bitcast.16, bf16[2,23,96,368]{3,2,1,0:T(8,128)(2,1)} %bitcast.17, bf16[6,128,768]{2,1,0:T(8,128)(2,1)} %constant.4.clone.lon_hbm, bf16[768,768]{1,0:T(8,128)(2,1)} %constant.5.clone.lat_hbm, ...), custom_call_target="tpu_custom_call" | custom-call | tf_op jit(solution)/shard_map/afno_backward/pallas_call | solution.py:548
  166.2 0.7 emit.1
  166.9 1.7 %copy.14 = bf16[1,96,23,768]{3,1,2,0:T(8,128)(2,1)} copy(bf16[1,96,23,768]{3,1,2,0:T(8,128)(2,1)S(1)} %bitcast.15) | data formatting | bytes 6782976

commit v4 on v3

--- a/solution.py
+++ b/solution.py
@@ -429,12 +429,14 @@
     zr[my_z] = zs[my_zl]
     send_back(3)
 
-    def finish(c, groups):
+    def finish(chunks, between=None):
+        groups = [group for c in chunks for group in CHUNKS[c]]
         size = ROWS * len(groups)
 
-        def unpack(g):
+        def unpack(c, g):
             lanes = 0
-            for i, group in enumerate(groups):
+            for group in CHUNKS[c]:
+                i = groups.index(group)
                 width = 2 * CP if group == ODD else PP
                 got = br[c][g, :, lanes : lanes + width].astype(F32)
                 for s in range(2):
@@ -467,22 +469,25 @@
                         work[pl.ds(at, HP, stride=size), :] = parts[k]
                 lanes += width
 
-        def arrived(peers):
-            for peer in peers:
-                backward[c][1](peer).wait_recv()
-
-        def two(i, carry):
-            peers = [lax.rem(me + G - 2 * i, G), lax.rem(me + G - 2 * i - 1, G)]
-            arrived(peers)
-            for peer in peers:
-                unpack(peer)
-            return carry
-
-        first = lax.rem(me + G - 1, G)
-        arrived([first])
-        unpack(me)
-        unpack(first)
-        lax.fori_loop(1, G // 2, two, 0)
+        def arrive(c):
+            def two(i, carry):
+                peers = [lax.rem(me + G - 2 * i, G), lax.rem(me + G - 2 * i - 1, G)]
+                for peer in peers:
+                    backward[c][1](peer).wait_recv()
+                for peer in peers:
+                    unpack(c, peer)
+                return carry
+
+            first = lax.rem(me + G - 1, G)
+            backward[c][1](first).wait_recv()
+            unpack(c, me)
+            unpack(c, first)
+            lax.fori_loop(1, G // 2, two, 0)
+
+        for c in chunks:
+            arrive(c)
+            if between is not None and c == chunks[0]:
+                between()
         table = lon_ref[groups[0] : groups[0] + len(groups)].reshape(size, W)
 
         def block(first, count):
@@ -492,9 +497,9 @@
                 columns.append(jnp.transpose(v)[:C])
             new = nn(jnp.concatenate(columns, 0), table).reshape(count, C, W) * SCALE
             at = pl.ds(first, count)
-            if c == 0:
+            if chunks[0] == 0:
                 acc[at] = x_ref[at, :C].astype(F32) + new
-            elif c < len(CHUNKS) - 1:
+            elif chunks[-1] < len(CHUNKS) - 1:
                 acc[at] += new
             else:
                 out_ref[at] = (acc[at] + new).astype(BF16)
@@ -510,18 +515,22 @@
         over_peers(me, lambda peer, c=c: forward[c][0](peer).wait_send())
     over_peers(my_yc, lambda peer: yc_copy(peer, my_yc).wait_send(), 1, 8)
     over_peers(my_x, lambda peer: x_copy(peer, my_x).wait_send(), 1, 4)
-    for c in range(3):
-        finish(c, CHUNKS[c])
+    def share():
+        over_peers(my_z, lambda peer: z_copy(peer, peer).wait_recv(), -1, 8)
+        ts[...] = jnp.sum(zr[...], axis=0)
+        over_peers(my_x, lambda peer: share_copy(peer, my_x).start(), 1, 4)
+        tr[my_x] = ts[...]
+
+    finish((0,))
+    finish((1,))
+    for c in range(2):
+        over_peers(me, lambda peer, c=c: backward[c][0](peer).wait_send())
+    finish((2, 3), share)
+    over_peers(my_x, lambda peer: share_copy(peer, peer).wait_recv(), -1, 4)
+    g_ref[...] = tr[...]
+    for c in range(2, 4):
         over_peers(me, lambda peer, c=c: backward[c][0](peer).wait_send())
     over_peers(my_z, lambda peer: z_copy(peer, my_z).wait_send(), 1, 8)
-    over_peers(my_z, lambda peer: z_copy(peer, peer).wait_recv(), -1, 8)
-    ts[...] = jnp.sum(zr[...], axis=0)
-    over_peers(my_x, lambda peer: share_copy(peer, my_x).start(), 1, 4)
-    tr[my_x] = ts[...]
-    finish(3, CHUNKS[3])
-    over_peers(my_x, lambda peer: share_copy(peer, peer).wait_recv(), -1, 4)
-    g_ref[...] = tr[...]
-    over_peers(me, lambda peer: backward[3][0](peer).wait_send())
     over_peers(my_x, lambda peer: share_copy(peer, my_x).wait_send(), 1, 4)
 
 

time: 169 us -> 167 us (0.988)
  no operation moved by 1% of the time
where the time goes in v4:
time: 167 us
  Pallas kernels  165 us (99%)
  local copies, waits for them, and re-layouts  1.74 us (1%)
    pallas_call x1, Pallas kernels, on_device(): pl.pallas_call(kernel, out_shape=(pltpu.VMEM((HL, C, W), BF16), pltpu.VME...  164 us

profile of v4, /device:TPU:32, one launch (start us, length us, event | category | flops | bytes accessed | tf_op | source)
XLA Modules:
  0.0 167.1 jit_solution(17191603392724789383)
XLA Ops:
  0.6 164.0 %afno_backward.1 = (bf16[23,96,768]{2,1,0:T(8,128)(2,1)S(1)}, f32[4,8,128]{2,1,0:T(8,128)S(1)}) custom-call(bf16[23,96,768]{2,1,0:T(8,128)(2,1)} %bitcast.16, bf16[2,23,96,368]{3,2,1,0:T(8,128)(2,1)} %bitcast.17, bf16[6,128,768]{2,1,0:T(8,128)(2,1)} %constant.4.clone.lon_hbm, bf16[768,768]{1,0:T(8,128)(2,1)} %constant.5.clone.lat_hbm, ...), custom_call_target="tpu_custom_call" | custom-call | tf_op jit(solution)/shard_map/afno_backward/pallas_call | solution.py:557
  164.6 0.7 emit.1
  165.3 1.7 %copy.14 = bf16[1,96,23,768]{3,1,2,0:T(8,128)(2,1)} copy(bf16[1,96,23,768]{3,1,2,0:T(8,128)(2,1)S(1)} %bitcast.15) | data formatting | bytes 6782976

commit v5 on v4

--- a/solution.py
+++ b/solution.py
@@ -333,7 +333,7 @@
         for group in groups:
             if group == ODD:
                 got = fr[c][:, :, : 2 * CP].reshape(G * MSG, 2 * CP)
-                got = jnp.concatenate([got, rem[...].astype(BF16)], 1)
+                got = jnp.concatenate([got, rem[: G * MSG].astype(BF16)], 1)
             else:
                 got = fr[c][:, :, lanes : lanes + PP].reshape(G * MSG, PP)
             dz_ref[...] = tn(got, lat_ref[...])
@@ -454,7 +454,7 @@
                             few[s, 6 * q : 6 * q + 6, :] = v
 
                         spread(br[c], g, s, store)
-                        last = few[s]
+                        last = few[s, :HP]
                     else:
                         last = p[2]
                     parts.append(
@@ -575,14 +575,14 @@
             messages,
             messages,
             messages,
-            pltpu.VMEM((HP * MOST * ROWS, CP), F32),
+            pltpu.VMEM(((HP + 2) * MOST * ROWS, CP), F32),
             pltpu.VMEM((HL, C, W), F32),
             pltpu.VMEM((KG * C, 2 * PP), F32),
             pltpu.VMEM((KG * C, 2 * PP), BF16),
             pltpu.VMEM((G * MSG, PP), F32),
-            pltpu.VMEM((G * MSG, CP), F32),
+            pltpu.VMEM((G * MSG + 8, CP), F32),
             pltpu.VMEM((G, 2, 8, CP), F32),
-            pltpu.VMEM((2, HP, CP), F32),
+            pltpu.VMEM((2, HP + 8, CP), F32),
             pltpu.VMEM((KG, 2 * C, PP), BF16),
             pltpu.VMEM((2 * C, 2 * C), BF16),
             pltpu.VMEM((2 * C, 2 * C), BF16),

time: 167 us -> 167 us (level)
  no operation moved by 1% of the time
where the time goes in v5:
time: 167 us
  Pallas kernels  165 us (99%)
  local copies, waits for them, and re-layouts  1.74 us (1%)
    pallas_call x1, Pallas kernels, on_device(): pl.pallas_call(kernel, out_shape=(pltpu.VMEM((HL, C, W), BF16), pltpu.VME...  164 us

profile of v5, /device:TPU:32, one launch (start us, length us, event | category | flops | bytes accessed | tf_op | source)
XLA Modules:
  0.0 167.1 jit_solution(9234536420825255303)
XLA Ops:
  0.6 164.0 %afno_backward.1 = (bf16[23,96,768]{2,1,0:T(8,128)(2,1)S(1)}, f32[4,8,128]{2,1,0:T(8,128)S(1)}) custom-call(bf16[23,96,768]{2,1,0:T(8,128)(2,1)} %bitcast.16, bf16[2,23,96,368]{3,2,1,0:T(8,128)(2,1)} %bitcast.17, bf16[6,128,768]{2,1,0:T(8,128)(2,1)} %constant.4.clone.lon_hbm, bf16[768,768]{1,0:T(8,128)(2,1)} %constant.5.clone.lat_hbm, ...), custom_call_target="tpu_custom_call" | custom-call | tf_op jit(solution)/shard_map/afno_backward/pallas_call | solution.py:557
  164.6 0.7 emit.1
  165.3 1.7 %copy.14 = bf16[1,96,23,768]{3,1,2,0:T(8,128)(2,1)} copy(bf16[1,96,23,768]{3,1,2,0:T(8,128)(2,1)S(1)} %bitcast.15) | data formatting | bytes 6782976
